TPU v7x, 128 devices: a whole 4x4x4 slice. The times are simulated.
128 devices in a mesh: blk: 32 (over x, y, core), red: 4 (over z).
Axes of the slice: x: 4, y: 4, z: 4, core: 2. Of those that a mesh axis runs over, the one named last changes fastest.
Arguments:
- amplitudes: bfloat16 [16, 8, 1024, 1024], P('red', None, 'blk'), may hold values from -6 to 6
- dressed: bfloat16 [16, 8, 1024, 1024], P('red', None, 'blk'), may hold values from -0.125 to 0.125
- integrals: bfloat16 [8, 8, 1024, 1024], P(None, None, 'blk', 'red'), may hold values from -8 to 8
- occ_irrep: int32 [200], replicated, may hold values from 0 to 7
- virt_irrep: int32 [1024], replicated, may hold values from 0 to 7
- occ_energy: float32 [200], replicated, may hold values from -2 to -0.3
- virt_energy: float32 [1024], replicated, may hold values from 0.1 to 4
- slab_i: int32 [8], replicated, may hold values from 0 to 199
- slab_j: int32 [8], replicated, may hold values from 0 to 199
- slab_k: int32 [16], P('red'), may hold values from 0 to 199
Outputs:
- updated: float32 [8, 8, 1024, 1024], P(None, None, 'blk', 'red')
Inputs may be any that keep to these rules, and one draw needn't show every extreme that they name: `occ_irrep`: irrep labels of the eight irreps of D2h. `virt_irrep`: irrep labels of the eight irreps of D2h. `slab_i`: indices into the 200 occupied orbitals, repeats allowed. `slab_j`: indices into the 200 occupied orbitals, repeats allowed. `slab_k`: indices into the 200 occupied orbitals, repeats allowed.
All inputs are finite; a program needn't handle non-finite values.
Results may differ from a plain program's by a relative error of at most 0.0003.
Values may be sent and summed in bfloat16 or wider, within the bound.
No kernel may reach another device: no remote copies, remote signals or barrier semaphores. Data moves between devices by JAX's collectives and lax.ppermute only.
A program may use at most 192 MiB of HBM per device.

v0:
```python
import jax
import jax.numpy as jnp
import numpy as np
from jax import lax
from jax.sharding import PartitionSpec as P


def table_lookup(table, picks):
    hits = picks[:, None] == jnp.arange(table.shape[0], dtype=jnp.int32)[None, :]
    return jnp.sum(jnp.where(hits, table[None, :], jnp.zeros((), table.dtype)), axis=1)


def on_device(
    amplitudes,
    dressed,
    integrals,
    occ_irrep,
    virt_irrep,
    occ_energy,
    virt_energy,
    slab_i,
    slab_j,
    slab_k,
):
    blk_size = lax.axis_size("blk")
    red_size = lax.axis_size("red")
    k_local, slab_rows, virt_rows, virt_all = amplitudes.shape
    occ_cols = dressed.shape[1]
    cols_kept = virt_all // red_size
    pair_count = slab_rows * occ_cols // blk_size
    own_rows = max(1, pair_count // occ_cols)
    own_cols = min(pair_count, occ_cols)
    owners = np.arange(blk_size)
    first_pair = owners * pair_count
    table_rows = ((first_pair // occ_cols)[:, None] + np.arange(own_rows)[None, :]).reshape(-1)
    table_cols = ((first_pair % occ_cols)[:, None] + np.arange(own_cols)[None, :]).reshape(-1)
    blk_place = lax.axis_index("blk")
    red_place = lax.axis_index("red")
    label_i = table_lookup(occ_irrep, slab_i)
    label_j = table_lookup(occ_irrep, slab_j)
    label_k = table_lookup(occ_irrep, slab_k)
    rows_label = lax.dynamic_slice_in_dim(virt_irrep, blk_place * virt_rows, virt_rows)
    pair_virt = jnp.bitwise_xor(rows_label[:, None], virt_irrep[None, :])
    amp_sym = jnp.bitwise_xor(
        jnp.bitwise_xor(label_k[:, None], label_i[None, :])[:, :, None, None], pair_virt[None, None]
    )
    kept_amp = jnp.where(amp_sym == 0, amplitudes, jnp.zeros((), amplitudes.dtype))
    dre_sym = jnp.bitwise_xor(
        jnp.bitwise_xor(label_k[:, None], label_j[None, :])[:, :, None, None], pair_virt[None, None]
    )
    kept_dre = jnp.where(dre_sym == 0, dressed, jnp.zeros((), dressed.dtype))
    send_amp = jnp.take(kept_amp, table_rows, axis=1).reshape(
        k_local, blk_size, own_rows, virt_rows, virt_all
    )
    send_dre = jnp.take(kept_dre, table_cols, axis=1).reshape(
        k_local, blk_size, own_cols, virt_rows, virt_all
    )
    amp_owner, dre_owner = (
        lax.all_to_all(send_amp, "blk", split_axis=1, concat_axis=3, tiled=True),
        lax.all_to_all(send_dre, "blk", split_axis=1, concat_axis=3, tiled=True),
    )
    amp_owner = amp_owner[:, 0]
    dre_owner = dre_owner[:, 0]
    partial_cycle = jnp.einsum(
        "kiac,kjcb->ijab", amp_owner, dre_owner, preferred_element_type=jnp.float32
    )
    summed = lax.psum_scatter(partial_cycle, "red", scatter_dimension=3, tiled=True)
    cycle_pairs = summed.reshape(pair_count, virt_all, cols_kept)
    cycle_kept = lax.all_to_all(
        cycle_pairs, "blk", split_axis=1, concat_axis=0, tiled=True
    ).reshape(slab_rows, occ_cols, virt_rows, cols_kept)
    energy_i = table_lookup(occ_energy, slab_i)
    energy_j = table_lookup(occ_energy, slab_j)
    energy_a = lax.dynamic_slice_in_dim(virt_energy, blk_place * virt_rows, virt_rows)
    energy_b = lax.dynamic_slice_in_dim(virt_energy, red_place * cols_kept, cols_kept)
    label_b = lax.dynamic_slice_in_dim(virt_irrep, red_place * cols_kept, cols_kept)
    denom = (
        energy_i[:, None, None, None]
        + energy_j[None, :, None, None]
        - energy_a[None, None, :, None]
        - energy_b[None, None, None, :]
    )
    out_virt = jnp.bitwise_xor(rows_label[:, None], label_b[None, :])
    out_sym = jnp.bitwise_xor(
        jnp.bitwise_xor(label_i[:, None], label_j[None, :])[:, :, None, None], out_virt[None, None]
    )
    value = (integrals.astype(jnp.float32) + cycle_kept) / denom
    return jnp.where(out_sym == 0, value, jnp.zeros((), jnp.float32))


def solution(mesh):
    in_specs = (
        P("red", None, "blk", None),
        P("red", None, "blk", None),
        P(None, None, "blk", "red"),
        P(),
        P(),
        P(),
        P(),
        P(),
        P(),
        P("red"),
    )
    out_specs = P(None, None, "blk", "red")
    return jax.shard_map(
        on_device, mesh=mesh, in_specs=in_specs, out_specs=out_specs, check_vma=False
    )
```

profile of v0, /device:TPU:0, one launch (start us, length us, event | category | flops | bytes accessed | tf_op | source)
XLA Modules:
  0.0 594.6 jit_solution(14300901560016580379)
XLA Ops:
  6.5 0.8 dynamic_slice.12
  7.3 0.8 broadcast_xor_fusion
  8.1 0.7 pad_clamp_fusion
  8.7 0.9 select_reduce_fusion.4
  9.6 0.9 select_reduce_fusion.3
  10.5 0.1 broadcast_xor_fusion.3
  10.6 5.2 fusion.1
  15.8 6.6 %gather_fusion.1 = bf16[32,4,32,1024]{3,2,1,0:T(8,128)(2,1)} fusion(bf16[4,8,32,1024]{3,2,1,0:T(8,128)(2,1)} %get-tuple-element.9, s32[1024]{0:T(1024)S(1)} %pad_clamp_fusion), kind=kCustom, calls=%fused_computation.1 | custom fusion | bytes 16777344 | tf_op jit(solution)/shard_map/jit(_take)/gather | solution.py:52
  22.4 0.0 copy-start.4
  22.4 7.7 %all-to-all-start.1 = ((bf16[4,32,1,32,1024]{4,3,0,2,1:T(8,128)(2,1)}), bf16[4,32,1,32,1024]{4,3,0,2,1:T(8,128)(2,1)}, u32[]{:S(2)}, u32[]{:S(2)}) async-start(bf16[4,32,1,32,1024]{4,3,0,2,1:T(8,128)(2,1)} %bitcast.37), calls=%async_computation.1 | async-start | bytes 16777216 | tf_op jit(solution)/shard_map/all_to_all | solution.py:59
  30.0 0.0 copy-done.4
  30.1 7.2 %gather_fusion = bf16[64,4,32,1024]{3,2,1,0:T(8,128)(2,1)} fusion(bf16[4,8,32,1024]{3,2,1,0:T(8,128)(2,1)S(1)} %get-tuple-element.10, s32[1024]{0:T(1024)S(1)} %pad_clamp_fusion.1), kind=kCustom, calls=%fused_computation | custom fusion | bytes 33554688 | tf_op jit(solution)/shard_map/jit(_take)/gather | solution.py:55
  37.3 14.2 %copy.40 = bf16[4,32,2,32,1024]{4,3,2,0,1:T(8,128)(2,1)} copy(bf16[4,32,2,32,1024]{4,3,0,2,1:T(8,128)(2,1)} %bitcast.36) | data formatting | bytes 33554432 | tf_op jit(solution)/shard_map/jit(_take)/gather | solution.py:55
  51.5 92.3 %all-to-all-done.1 = bf16[4,32,1,32,1024]{4,3,0,2,1:T(8,128)(2,1)} async-done(((bf16[4,32,1,32,1024]{4,3,0,2,1:T(8,128)(2,1)}), bf16[4,32,1,32,1024]{4,3,0,2,1:T(8,128)(2,1)}, u32[]{:S(2)}, u32[]{:S(2)}) %all-to-all-start.1) | async-done | bytes 8388640 | tf_op jit(solution)/shard_map/all_to_all | solution.py:59
  143.7 16.3 %all-to-all-start = ((bf16[4,32,2,32,1024]{4,3,2,0,1:T(8,128)(2,1)}), bf16[4,32,2,32,1024]{4,3,2,0,1:T(8,128)(2,1)}, u32[]{:S(2)}, u32[]{:S(2)}) async-start(bf16[4,32,2,32,1024]{4,3,2,0,1:T(8,128)(2,1)} %copy.40), calls=%async_computation | async-start | bytes 33554432 | tf_op jit(solution)/shard_map/all_to_all | solution.py:60
  160.1 0.0 reduce-scatter.2.cloned.1.call-start
  160.1 8.5 %copy.43 = bf16[4,32,1,32,1024]{4,3,1,0,2:T(8,128)(2,1)} copy(bf16[4,32,1,32,1024]{4,3,0,2,1:T(8,128)(2,1)} %all-to-all-done.1) | data formatting | bytes 16777216 | tf_op jit(solution)/shard_map/all_to_all | solution.py:59
  168.6 232.4 %all-to-all-done = bf16[4,32,2,32,1024]{4,3,2,0,1:T(8,128)(2,1)} async-done(((bf16[4,32,2,32,1024]{4,3,2,0,1:T(8,128)(2,1)}), bf16[4,32,2,32,1024]{4,3,2,0,1:T(8,128)(2,1)}, u32[]{:S(2)}, u32[]{:S(2)}) %all-to-all-start) | async-done | bytes 16777248 | tf_op jit(solution)/shard_map/all_to_all | solution.py:60
  401.0 8.3 %copy.41 = bf16[4,32,2,32,1024]{4,3,1,2,0:T(8,128)(2,1)S(1)} copy(bf16[4,32,2,32,1024]{4,3,2,0,1:T(8,128)(2,1)} %all-to-all-done) | data formatting | bytes 33554432 | tf_op jit(solution)/shard_map/all_to_all | solution.py:60
  409.3 24.3 %convolution_bitcast_fusion = f32[1,2,1024,1024]{2,3,1,0:T(8,128)} fusion(bf16[4,2,1024,1024]{3,2,1,0:T(8,128)(2,1)S(1)} %bitcast.38, bf16[4,1024,1024,1]{2,1,3,0:T(8,128)(2,1)} %bitcast.39), kind=kOutput, calls=%fused_computation.6 | convolution fusion | flops 17179869184 | bytes 33554432 | tf_op jit(solution)/shard_map/kiac,kjcb->ijab/dot_general | solution.py:64
  433.6 0.0 reduce-scatter.2.cloned.1.call-update
  433.6 110.5 %reduce-scatter.2.cloned.1.call-done = f32[1,2,1024,256]{2,3,1,0:T(8,128)} async-done(((f32[1,2,1024,1024]{2,3,1,0:T(8,128)}), f32[1,2,1024,256]{2,3,1,0:T(8,128)}) %reduce-scatter.2.cloned.1.call-update) | async-done | bytes 2097168 | tf_op jit(solution)/shard_map/reduce_scatter | solution.py:67
  544.1 4.1 copy.45
  548.3 0.0 copy-start.1
  548.3 0.0 copy-start.2
  548.3 0.0 copy-start.3
  548.3 7.2 %all-to-all-start.2 = ((f32[2,1024,256]{2,0,1:T(2,128)}), f32[2,1024,256]{2,0,1:T(2,128)S(1)}, u32[]{:S(2)}, u32[]{:S(2)}) async-start(f32[2,1024,256]{2,0,1:T(2,128)} %copy.45), calls=%async_computation.3 | async-start | bytes 4194304 | tf_op jit(solution)/shard_map/all_to_all | solution.py:69
  555.5 0.8 dynamic_slice.13
  556.3 0.8 dynamic_slice.14
  557.0 0.8 dynamic_slice.15
  557.8 0.0 copy-done.1
  557.8 0.0 copy-done.2
  557.8 0.0 copy-done.3
  557.8 0.2 select_reduce_fusion.1
  558.0 0.1 broadcast_xor_fusion.2
  558.1 0.1 broadcast_add_fusion
  558.2 0.1 broadcast_xor_fusion.1
  558.2 0.1 broadcast_subtract_fusion
  558.3 26.1 %all-to-all-done.2 = f32[2,1024,256]{2,0,1:T(2,128)S(1)} async-done(((f32[2,1024,256]{2,0,1:T(2,128)}), f32[2,1024,256]{2,0,1:T(2,128)S(1)}, u32[]{:S(2)}, u32[]{:S(2)}) %all-to-all-start.2) | async-done | bytes 2097184 | tf_op jit(solution)/shard_map/all_to_all | solution.py:69
  584.4 0.2 copy.46
  584.6 0.0 copy-start
  584.6 0.1 copy.47
  584.8 1.1 copy-done
  585.8 2.0 fusion.3
  (1 shorter events, 0.0 us)
Async XLA Ops:
  22.4 7.7 %copy-start.4 = (s32[64]{0:T(128)S(1)}, s32[64]{0:T(128)}, u32[]{:S(2)}) copy-start(s32[64]{0:T(128)} %constant.73) | copy-start | bytes 772
  22.4 121.4 %all-to-all-start.1 = ((bf16[4,32,1,32,1024]{4,3,0,2,1:T(8,128)(2,1)}), bf16[4,32,1,32,1024]{4,3,0,2,1:T(8,128)(2,1)}, u32[]{:S(2)}, u32[]{:S(2)}) async-start(bf16[4,32,1,32,1024]{4,3,0,2,1:T(8,128)(2,1)} %bitcast.37), calls=%async_computation.1 | async-start | bytes 16777216 | tf_op jit(solution)/shard_map/all_to_all | solution.py:59
  143.7 257.2 %all-to-all-start = ((bf16[4,32,2,32,1024]{4,3,2,0,1:T(8,128)(2,1)}), bf16[4,32,2,32,1024]{4,3,2,0,1:T(8,128)(2,1)}, u32[]{:S(2)}, u32[]{:S(2)}) async-start(bf16[4,32,2,32,1024]{4,3,2,0,1:T(8,128)(2,1)} %copy.40), calls=%async_computation | async-start | bytes 33554432 | tf_op jit(solution)/shard_map/all_to_all | solution.py:60
  160.1 384.1 %reduce-scatter.2.cloned.1.call-start = ((), (), s32[]{:S(2)}) async-start(), calls=%async_computation.4 | async-start | bytes 10485760 | tf_op jit(solution)/shard_map/reduce_scatter | solution.py:67
  548.3 9.5 %copy-start.1 = (s32[8]{0:T(128)S(1)}, s32[8]{0:T(128)}, u32[]{:S(2)}) copy-start(s32[8]{0:T(128)} %param.19) | copy-start | bytes 100
  548.3 9.5 %copy-start.2 = (s32[8]{0:T(128)S(1)}, s32[8]{0:T(128)}, u32[]{:S(2)}) copy-start(s32[8]{0:T(128)} %param.20) | copy-start | bytes 100
  548.3 9.5 %copy-start.3 = (f32[200]{0:T(256)S(1)}, f32[200]{0:T(256)}, u32[]{:S(2)}) copy-start(f32[200]{0:T(256)} %param.17) | copy-start | bytes 2404
  548.3 36.2 %all-to-all-start.2 = ((f32[2,1024,256]{2,0,1:T(2,128)}), f32[2,1024,256]{2,0,1:T(2,128)S(1)}, u32[]{:S(2)}, u32[]{:S(2)}) async-start(f32[2,1024,256]{2,0,1:T(2,128)} %copy.45), calls=%async_computation.3 | async-start | bytes 4194304 | tf_op jit(solution)/shard_map/all_to_all | solution.py:69
  584.6 1.2 copy-start
Sparse Core Ops, SparseCore 0:
  433.7 110.3 reduce-scatter.1
where the time goes:
time: 596 us; the launch traced here: 595 us
  waiting for transfers between devices  461 us (77%)
  local copies, waits for them, and re-layouts  53.3 us (9%)
  starting transfers between devices  31.3 us (5%)
  matrix products  24.3 us (4%)
  between operations  13.5 us (2%)
  other arithmetic  10.9 us (2%)
    all_to_all x1, waiting for transfers between devices, on_device(): lax.all_to_all(send_dre, 'blk', split_axis=1, concat_axis=3, tiled=True)  232 us
    reduce_scatter x1, waiting for transfers between devices, on_device(): lax.psum_scatter(partial_cycle, 'red', scatter_dimension=3, tiled=True)  111 us
    all_to_all x1, waiting for transfers between devices, on_device(): lax.all_to_all(send_amp, 'blk', split_axis=1, concat_axis=3, tiled=True)  92.3 us
    all_to_all x1, waiting for transfers between devices, on_device(): lax.all_to_all(cycle_pairs, 'blk', split_axis=1, concat_axis=0, tiled=True)  26.1 us
    dot_general x1, matrix products, on_device(): jnp.einsum('kiac,kjcb->ijab', amp_owner, dre_owner, preferred_element_typ...  24.3 us
    gather x2, local copies, waits for them, and re-layouts, on_device(): jnp.take(kept_dre, table_cols, axis=1)  21.4 us
    all_to_all x1, starting transfers between devices, on_device(): lax.all_to_all(send_dre, 'blk', split_axis=1, concat_axis=3, tiled=True)  16.3 us
  transfers between devices with their start and end apart: 4, of which 4 were waited for; matrix products, arithmetic and copies ran while one was open for 5% of the time, Pallas kernels for 0%

commit v1 on v0

--- a/solution.py
+++ b/solution.py
@@ -1,8 +1,22 @@
+import functools
+
 import jax
 import jax.numpy as jnp
 import numpy as np
 from jax import lax
+from jax.experimental import pallas as pl
+from jax.experimental.pallas import tpu as pltpu
 from jax.sharding import PartitionSpec as P
+
+F32 = jnp.float32
+BF16 = jnp.bfloat16
+I32 = jnp.int32
+
+RING = 4
+CORES = 2
+WIDE = 192
+PART = 64
+NT = (((1,), (1,)), ((), ()))
 
 
 def table_lookup(table, picks):
@@ -10,7 +24,7 @@
     return jnp.sum(jnp.where(hits, table[None, :], jnp.zeros((), table.dtype)), axis=1)
 
 
-def on_device(
+def dense_form(
     amplitudes,
     dressed,
     integrals,
@@ -55,12 +69,8 @@
     send_dre = jnp.take(kept_dre, table_cols, axis=1).reshape(
         k_local, blk_size, own_cols, virt_rows, virt_all
     )
-    amp_owner, dre_owner = (
-        lax.all_to_all(send_amp, "blk", split_axis=1, concat_axis=3, tiled=True),
-        lax.all_to_all(send_dre, "blk", split_axis=1, concat_axis=3, tiled=True),
-    )
-    amp_owner = amp_owner[:, 0]
-    dre_owner = dre_owner[:, 0]
+    amp_owner = lax.all_to_all(send_amp, "blk", split_axis=1, concat_axis=3, tiled=True)[:, 0]
+    dre_owner = lax.all_to_all(send_dre, "blk", split_axis=1, concat_axis=3, tiled=True)[:, 0]
     partial_cycle = jnp.einsum(
         "kiac,kjcb->ijab", amp_owner, dre_owner, preferred_element_type=jnp.float32
     )
@@ -88,6 +98,451 @@
     return jnp.where(out_sym == 0, value, jnp.zeros((), jnp.float32))
 
 
+def coords():
+    blk = lax.axis_index("blk")
+    return blk // (RING * CORES), (blk // CORES) % RING, blk % CORES, lax.axis_index("red")
+
+
+def iota(shape, dim):
+    return lax.broadcasted_iota(I32, shape, dim)
+
+
+def picked_column(row, first, count):
+    wide = row.shape[1]
+    hit = iota((count, wide), 1) == iota((count, wide), 0) + first
+    kept = jnp.where(hit, jnp.broadcast_to(row.astype(F32), (count, wide)), 0.0)
+    return jnp.sum(kept, axis=1, keepdims=True).astype(row.dtype)
+
+
+def rank_kernel(lv_ref, rank_ref, part_ref, fits_ref):
+    wide = lv_ref.shape[1]
+    quarter = wide // RING
+    tri = (iota((quarter, quarter), 0) < iota((quarter, quarter), 1)).astype(F32).astype(BF16)
+    base = jnp.zeros((16, 1), F32)
+    most_part = jnp.zeros((1, 1), F32)
+    for part in range(RING):
+        lanes = slice(part * quarter, (part + 1) * quarter)
+        member = (iota((16, quarter), 0) == lv_ref[:, lanes]).astype(F32)
+        before = jnp.dot(member.astype(BF16), tri, preferred_element_type=F32)
+        part_ref[:, lanes] = jnp.sum(member * before, axis=0, keepdims=True).astype(I32)
+        rank_ref[:, lanes] = jnp.sum(member * (before + base), axis=0, keepdims=True).astype(I32)
+        count = jnp.sum(member, axis=1, keepdims=True)
+        most_part = jnp.maximum(most_part, jnp.max(count))
+        base = base + count
+    fits = jnp.logical_and(jnp.max(base) <= WIDE, jnp.max(most_part) <= PART)
+    fits_ref[0] = fits.astype(I32)
+
+
+def pack_kernel(
+    occ_ref,
+    si_ref,
+    sj_ref,
+    sk_ref,
+    lv_ref,
+    rank_ref,
+    part_ref,
+    amp_ref,
+    dre_ref,
+    pa_ref,
+    pb0_ref,
+    pb1_ref,
+    pb2_ref,
+    pb3_ref,
+    hot_main,
+    hot_low,
+    hot_high,
+    hot_part,
+    own_label,
+    kept,
+):
+    _, y, _, z = coords()
+    k = pl.program_id(0)
+    rows, wide = amp_ref.shape[2:]
+    half = hot_main.shape[0]
+
+    @pl.when(k == 0)
+    def _():
+        rank = rank_ref[...]
+        slot = iota((half, wide), 0)
+        hot_main[...] = (slot == rank).astype(F32).astype(BF16)
+        hot_low[...] = jnp.logical_and(slot + half == rank, slot < PART).astype(F32).astype(BF16)
+        hot_high[...] = (
+            jnp.logical_and(slot + half - PART == rank, slot >= PART).astype(F32).astype(BF16)
+        )
+        step = (iota((1, wide), 1) // (wide // RING) - z + RING) % RING
+        hot_part[...] = (
+            (iota((RING * PART, wide), 0) == step * PART + part_ref[...]).astype(F32).astype(BF16)
+        )
+        own_label[...] = picked_column(lv_ref[...], lax.axis_index("blk") * rows, rows)
+
+    lv = lv_ref[...]
+    lk = occ_ref[sk_ref[k]]
+
+    def put(at, label, block):
+        keep = jnp.bitwise_xor(own_label[...], jnp.bitwise_xor(lk, label)) == lv
+        kept[at * rows : (at + 1) * rows, :] = jnp.where(keep, block.astype(F32), 0.0).astype(BF16)
+
+    n_i = amp_ref.shape[1]
+    for i in range(n_i):
+        put(i, occ_ref[si_ref[i]], amp_ref[0, i])
+    main = lax.dot_general(kept[...], hot_main[...], NT, preferred_element_type=F32)
+    pa_ref[0, :n_i] = main.astype(BF16).reshape(n_i, rows, half)
+    lower = n_i * rows // 2
+    rest = lax.dot_general(kept[:lower], hot_low[...], NT, preferred_element_type=F32)
+    rest += lax.dot_general(kept[lower:], hot_high[...], NT, preferred_element_type=F32)
+    pa_ref[0, n_i:] = rest.astype(BF16).reshape(n_i // 2, rows, half)
+
+    for d in range(RING):
+        for jj in range(CORES):
+            j = ((y + d) % RING) * CORES + jj
+            put(jj * RING + d, occ_ref[sj_ref[j]], dre_ref[0, j])
+    packed = lax.dot_general(kept[...], hot_part[...], NT, preferred_element_type=F32)
+    for d, out in enumerate((pb0_ref, pb1_ref, pb2_ref, pb3_ref)):
+        even = packed[d * rows : (d + 1) * rows]
+        odd = packed[(RING + d) * rows : (RING + d + 1) * rows]
+        pieces = []
+        for s in range(RING):
+            pieces += [even[:, s * PART : (s + 1) * PART], odd[:, s * PART : (s + 1) * PART]]
+        out[0] = jnp.concatenate(pieces, axis=1).astype(BF16)
+
+
+def unpack_kernel(
+    occ_ref, si_ref, sk_ref, lv_ref, rank_ref, p0, p1, p2, p3, out_ref, hot_low, hot_high, order, labels
+):
+    x, y, core, _ = coords()
+    k = pl.program_id(0)
+    n_rest, rows, half = p0.shape[1:]
+    n_i = n_rest * 2 // 3
+    wide = lv_ref.shape[1]
+
+    @pl.when(k == 0)
+    def _():
+        p = iota((1, wide), 1)
+        source = (
+            ((x - (p // 128) % RING + RING) % RING) * (rows * 8)
+            + ((y - (p // rows) % RING + RING) % RING) * (rows * 2)
+            + jnp.bitwise_xor(core, p // (wide // 2)) * rows
+            + p % rows
+        )
+        pick = (iota((wide, wide), 0) == source).astype(F32).astype(BF16)
+        which = iota((16, wide), 0)
+        both = jnp.where(
+            which == 0,
+            jnp.broadcast_to(lv_ref[...], (16, wide)),
+            jnp.broadcast_to(jnp.minimum(rank_ref[...], 255), (16, wide)),
+        )
+        moved = jnp.dot(both.astype(F32).astype(BF16), pick, preferred_element_type=F32).astype(I32)
+        order[...] = moved[0:1]
+        rank = moved[1:2]
+        slot = iota((half, wide), 0)
+        main = (slot == rank).astype(F32).astype(BF16)
+        hot_low[:half] = main
+        hot_high[:half] = main
+        hot_low[half:] = jnp.logical_and(slot + half == rank, slot < PART).astype(F32).astype(BF16)
+        hot_high[half:] = (
+            jnp.logical_and(slot + half - PART == rank, slot >= PART).astype(F32).astype(BF16)
+        )
+        for d in range(RING):
+            first = x * (rows * 8) + ((y - d + RING) % RING) * (rows * 2) + core * rows
+            labels[d] = picked_column(lv_ref[...], first, rows)
+
+    lk = occ_ref[sk_ref[k]]
+    group = n_i // 2
+    for d, block in enumerate((p0, p1, p2, p3)):
+        rest = block[0, n_i:].reshape(group * rows, half)
+        for side, hot in enumerate((hot_low, hot_high)):
+            main = block[0, side * group : (side + 1) * group].reshape(group * rows, half)
+            spread = jnp.dot(
+                jnp.concatenate([main, rest], axis=1), hot[...], preferred_element_type=F32
+            )
+            for g in range(group):
+                i = side * group + g
+                label = jnp.bitwise_xor(lk, occ_ref[si_ref[i]])
+                keep = jnp.bitwise_xor(labels[d], label) == order[...]
+                at = (d * n_i + i) * rows
+                out_ref[0, at : at + rows, :] = jnp.where(
+                    keep, spread[g * rows : (g + 1) * rows], 0.0
+                ).astype(BF16)
+
+
+def cycle_kernel(a_ref, b0, b1, b2, b3, b4, b5, b6, b7, o0, o1, o2, o3, b_all, total):
+    k = pl.program_id(0)
+    depth = b0.shape[0] * b0.shape[2]
+    for n, b in enumerate((b0, b1, b2, b3, b4, b5, b6, b7)):
+        b_all[n * depth : (n + 1) * depth, :] = b[:, 0].reshape(depth, b.shape[3])
+    rows = a_ref.shape[1]
+    step = rows // 4
+    lanes = o0.shape[1]
+    for r in range(4):
+        at = slice(r * step, (r + 1) * step)
+        term = jnp.dot(a_ref[0, at], b_all[...], preferred_element_type=F32)
+
+        @pl.when(k == 0)
+        def _():
+            total[at] = term
+
+        @pl.when(jnp.logical_and(k > 0, k < pl.num_programs(0) - 1))
+        def _():
+            total[at] += term
+
+        @pl.when(k == pl.num_programs(0) - 1)
+        def _():
+            full = total[at] + term
+            for d, out in enumerate((o0, o1, o2, o3)):
+                out[at] = full[:, d * lanes : (d + 1) * lanes]
+
+
+def sum_kernel(o0, o1, o2, o3, s0, s1, s2, s3):
+    rows = s0.shape[0] * s0.shape[1]
+    for d, out in enumerate((s0, s1, s2, s3)):
+        at = slice(d * rows, (d + 1) * rows)
+        full = ((o0[at] + o1[at]) + o2[at]) + o3[at]
+        out[...] = full.reshape(out.shape)
+
+
+def update_kernel(
+    occ_ref,
+    si_ref,
+    sj_ref,
+    oe_ref,
+    lv_ref,
+    ve_ref,
+    part_ref,
+    t0,
+    t1,
+    t2,
+    t3,
+    int_ref,
+    out_ref,
+    hot,
+    own_label,
+    own_energy,
+):
+    _, y, _, z = coords()
+    i = pl.program_id(0)
+    rows, lanes = t0.shape[1:]
+    kept = int_ref.shape[3]
+    cols = pl.ds(pl.multiple_of(z * kept, kept), kept)
+
+    @pl.when(i == 0)
+    def _():
+        slot = iota((lanes, kept), 0)
+        part = part_ref[:, cols]
+        for jj in range(CORES):
+            hot[:, jj * kept : (jj + 1) * kept] = (
+                (slot == part + jj * PART).astype(F32).astype(BF16)
+            )
+        first = lax.axis_index("blk") * rows
+        own_label[...] = picked_column(lv_ref[...], first, rows)
+        own_energy[...] = picked_column(ve_ref[...], first, rows)
+
+    x = jnp.concatenate([t[0] for t in (t0, t1, t2, t3)], axis=0)
+    top = x.astype(BF16)
+    left = x - top.astype(F32)
+    mid = left.astype(BF16)
+    low = (left - mid.astype(F32)).astype(BF16)
+    count = RING * rows
+    three = jnp.dot(
+        jnp.concatenate([top, mid, low], axis=0), hot[...], preferred_element_type=F32
+    )
+    cycle = (three[:count] + three[count : 2 * count]) + three[2 * count :]
+    label_i = occ_ref[si_ref[i]]
+    energy_i = oe_ref[si_ref[i]]
+    label_b = lv_ref[:, cols]
+    energy_b = ve_ref[:, cols]
+    for d in range(RING):
+        for jj in range(CORES):
+            j = ((y + d) % RING) * CORES + jj
+            label = jnp.bitwise_xor(label_i, occ_ref[sj_ref[j]])
+            denom = ((energy_i + oe_ref[sj_ref[j]]) - own_energy[...]) - energy_b
+            term = cycle[d * rows : (d + 1) * rows, jj * kept : (jj + 1) * kept]
+            value = (int_ref[0, j].astype(F32) + term) / denom
+            keep = jnp.bitwise_xor(own_label[...], label) == label_b
+            out_ref[0, j] = jnp.where(keep, value, 0.0)
+
+
+SMEM = pl.BlockSpec(memory_space=pltpu.SMEM)
+
+
+def whole(shape):
+    return pl.BlockSpec(shape, lambda n: (0,) * len(shape))
+
+
+def cost(flops, moved):
+    return pl.CostEstimate(flops=flops, bytes_accessed=moved, transcendentals=0)
+
+
+def ranks(lv):
+    wide = lv.shape[1]
+    row = jax.ShapeDtypeStruct((1, wide), I32)
+    return pl.pallas_call(
+        rank_kernel,
+        out_shape=(row, row, jax.ShapeDtypeStruct((1,), I32)),
+        in_specs=[pl.BlockSpec(memory_space=pltpu.VMEM)],
+        out_specs=(
+            pl.BlockSpec(memory_space=pltpu.VMEM),
+            pl.BlockSpec(memory_space=pltpu.VMEM),
+            SMEM,
+        ),
+        name="ranks",
+    )(lv)
+
+
+def ring_x(d):
+    return [
+        (8 * x + m, 8 * ((x + d) % RING) + m) for x in range(RING) for m in range(RING * CORES)
+    ]
+
+
+def ring_y(d):
+    return [
+        (8 * x + 2 * y + c, 8 * x + 2 * ((y + d) % RING) + c)
+        for x in range(RING)
+        for y in range(RING)
+        for c in range(CORES)
+    ]
+
+
+def ring_z(d):
+    return [(z, (z + d) % RING) for z in range(RING)]
+
+
+def other_core():
+    return [(b, b ^ 1) for b in range(RING * RING * CORES)]
+
+
+def packed_form(
+    rank,
+    part,
+    amplitudes,
+    dressed,
+    integrals,
+    occ_irrep,
+    virt_irrep,
+    occ_energy,
+    virt_energy,
+    slab_i,
+    slab_j,
+    slab_k,
+):
+    n_k, n_i, rows, wide = amplitudes.shape
+    n_j = dressed.shape[1]
+    kept = integrals.shape[3]
+    half = 128
+    n_rest = n_i + n_i // 2
+    n_cols = RING * CORES * PART
+    lv = virt_irrep.reshape(1, wide)
+    ve = virt_energy.reshape(1, wide)
+    row_spec = whole((1, wide))
+    params = pltpu.CompilerParams(vmem_limit_bytes=48 * 1024 * 1024)
+
+    pa, *pb = pl.pallas_call(
+        pack_kernel,
+        grid=(n_k,),
+        out_shape=[jax.ShapeDtypeStruct((n_k, n_rest, rows, half), BF16)]
+        + [jax.ShapeDtypeStruct((n_k, rows, n_cols), BF16)] * RING,
+        in_specs=[SMEM] * 4
+        + [row_spec] * 3
+        + [pl.BlockSpec((1, n_i, rows, wide), lambda k: (k, 0, 0, 0))] * 2,
+        out_specs=[pl.BlockSpec((1, n_rest, rows, half), lambda k: (k, 0, 0, 0))]
+        + [pl.BlockSpec((1, rows, n_cols), lambda k: (k, 0, 0))] * RING,
+        scratch_shapes=[
+            pltpu.VMEM((half, wide), BF16),
+            pltpu.VMEM((half, wide), BF16),
+            pltpu.VMEM((half, wide), BF16),
+            pltpu.VMEM((RING * PART, wide), BF16),
+            pltpu.VMEM((rows, 1), I32),
+            pltpu.VMEM((n_i * rows, wide), BF16),
+        ],
+        compiler_params=params,
+        cost_estimate=cost(2 * 2 * n_k * n_i * rows * wide * 256, 5 << 20),
+        name="pack",
+    )(occ_irrep, slab_i, slab_j, slab_k, lv, rank, part, amplitudes, dressed)
+
+    pb_y = [pb[0]] + [lax.ppermute(pb[d], "blk", ring_y(d)) for d in (1, 3, 2)]
+    pb_y = [pb_y[0], pb_y[1], pb_y[3], pb_y[2]]
+    mine = jnp.stack(pb_y)
+    pa_y = [pa] + [lax.ppermute(pa, "blk", ring_y(d)) for d in (1, 2, 3)]
+    across = [mine] + [lax.ppermute(mine, "blk", ring_x(d)) for d in (1, 2, 3)]
+    twin = [lax.ppermute(b, "blk", other_core()) for b in across]
+
+    m_rows = RING * n_i * rows
+    spread = pl.pallas_call(
+        unpack_kernel,
+        grid=(n_k,),
+        out_shape=jax.ShapeDtypeStruct((n_k, m_rows, wide), BF16),
+        in_specs=[SMEM] * 3
+        + [row_spec] * 2
+        + [pl.BlockSpec((1, n_rest, rows, half), lambda k: (k, 0, 0, 0))] * RING,
+        out_specs=pl.BlockSpec((1, m_rows, wide), lambda k: (k, 0, 0)),
+        scratch_shapes=[
+            pltpu.VMEM((2 * half, wide), BF16),
+            pltpu.VMEM((2 * half, wide), BF16),
+            pltpu.VMEM((1, wide), I32),
+            pltpu.VMEM((RING, rows, 1), I32),
+        ],
+        compiler_params=params,
+        cost_estimate=cost(2 * n_k * m_rows * wide * 256, 10 << 20),
+        name="unpack",
+    )(occ_irrep, slab_i, slab_k, lv, rank, *pa_y)
+
+    parts = pl.pallas_call(
+        cycle_kernel,
+        grid=(n_k,),
+        out_shape=[jax.ShapeDtypeStruct((m_rows, CORES * PART), F32)] * RING,
+        in_specs=[pl.BlockSpec((1, m_rows, wide), lambda k: (k, 0, 0))]
+        + [pl.BlockSpec((RING, 1, rows, n_cols), lambda k: (0, k, 0, 0))] * 8,
+        out_specs=[pl.BlockSpec((m_rows, CORES * PART), lambda k: (0, 0))] * RING,
+        scratch_shapes=[pltpu.VMEM((wide, n_cols), BF16), pltpu.VMEM((m_rows, n_cols), F32)],
+        compiler_params=params,
+        cost_estimate=cost(2 * n_k * m_rows * wide * n_cols, 14 << 20),
+        name="cycle",
+    )(spread, *across, *twin)
+
+    sums = [parts[0]] + [lax.ppermute(parts[d], "red", ring_z(d)) for d in (1, 2, 3)]
+    terms = pl.pallas_call(
+        sum_kernel,
+        out_shape=[jax.ShapeDtypeStruct((n_i, rows, CORES * PART), F32)] * RING,
+        in_specs=[pl.BlockSpec(memory_space=pltpu.VMEM)] * RING,
+        out_specs=[pl.BlockSpec(memory_space=pltpu.VMEM)] * RING,
+        cost_estimate=cost(m_rows * 512, 3 << 20),
+        name="sums",
+    )(*sums)
+    back = [terms[0]] + [lax.ppermute(terms[d], "blk", ring_y(RING - d)) for d in (1, 2, 3)]
+
+    return pl.pallas_call(
+        update_kernel,
+        grid=(n_i,),
+        out_shape=jax.ShapeDtypeStruct(integrals.shape, F32),
+        in_specs=[SMEM] * 4
+        + [row_spec] * 3
+        + [pl.BlockSpec((1, rows, CORES * PART), lambda i: (i, 0, 0))] * RING
+        + [pl.BlockSpec((1, n_j, rows, kept), lambda i: (i, 0, 0, 0))],
+        out_specs=pl.BlockSpec((1, n_j, rows, kept), lambda i: (i, 0, 0, 0)),
+        scratch_shapes=[
+            pltpu.VMEM((CORES * PART, CORES * kept), BF16),
+            pltpu.VMEM((rows, 1), I32),
+            pltpu.VMEM((rows, 1), F32),
+        ],
+        compiler_params=params,
+        cost_estimate=cost(2 * 3 * m_rows * 128 * 512, 4 << 20),
+        name="update",
+    )(occ_irrep, slab_i, slab_j, occ_energy, lv, ve, part, *back, integrals)
+
+
+def on_device(*args):
+    virt_irrep = args[4]
+    rank, part, fits = ranks(virt_irrep.reshape(1, -1))
+    return lax.cond(
+        fits[0] == 1,
+        lambda r, p, *a: packed_form(r, p, *a),
+        lambda r, p, *a: dense_form(*a),
+        rank,
+        part,
+        *args,
+    )
+
+
 def solution(mesh):
     in_specs = (
         P("red", None, "blk", None),

time: 596 us -> 125 us (0.21)
  waiting for transfers between devices: 461 us -> 49.1 us
  local copies, waits for them, and re-layouts: 53.3 us -> 4.84 us
  Pallas kernels: 0 us -> 28.2 us
  matrix products: 24.3 us -> 0 us
  other arithmetic: 10.9 us -> 0.07 us
    all_to_all x3 -> x0, waiting for transfers between devices: 351 us -> none  [the longest x1 232 us: on_device(): lax.all_to_all(send_dre, 'blk', split_axis=1, concat_axis=3, tiled=True)]
    reduce_scatter x1 -> x0, waiting for transfers between devices: 111 us -> none  [on_device(): lax.psum_scatter(partial_cycle, 'red', scatter_dimension=3, tiled=True)]
    ppermute x0 -> x19, waiting for transfers between devices: none -> 49.1 us  [the longest x3 22.1 us: packed_form(): lax.ppermute(parts[d], 'red', ring_z(d))]
    all_to_all x3 -> x0, starting transfers between devices: 31.2 us -> none  [the longest x1 16.3 us: on_device(): lax.all_to_all(send_dre, 'blk', split_axis=1, concat_axis=3, tiled=True)]
    ppermute x0 -> x19, starting transfers between devices: none -> 28.2 us  [the longest x3 6.57 us: packed_form(): lax.ppermute(parts[d], 'red', ring_z(d))]
    pallas_call x0 -> x6, Pallas kernels: none -> 28.2 us  [the longest x1 9.58 us: packed_form(): pl.pallas_call(cycle_kernel, grid=(n_k,), out_shape=[jax.ShapeDtypeStruct...]
    gather x3 -> x0, local copies, waits for them, and re-layouts: 28 us -> none  [the longest x2 21.4 us: on_device(): jnp.take(kept_dre, table_cols, axis=1)]
    dot_general x1 -> x0, matrix products: 24.3 us -> none  [on_device(): jnp.einsum('kiac,kjcb->ijab', amp_owner, dre_owner, preferred_element_typ...]
  transfers between devices with their start and end apart: 4 -> 19, of which waited for: 4 -> 10; matrix products, arithmetic and copies ran while one was open for 5% -> 0% of each run, Pallas kernels for 0% -> 5%
where the time goes in v1:
time: 125 us
  waiting for transfers between devices  49.1 us (39%)
  Pallas kernels  28.2 us (23%)
  starting transfers between devices  28.2 us (23%)
  between operations  14 us (11%)
  local copies, waits for them, and re-layouts  4.84 us (4%)
    ppermute x3, waiting for transfers between devices, packed_form(): lax.ppermute(parts[d], 'red', ring_z(d))  22.1 us
    ppermute x3, waiting for transfers between devices, packed_form(): pa_y = [pa] + [lax.ppermute(pa, 'blk', ring_y(d)) for d in (1, 2, 3)]  13.9 us
    pallas_call x1, Pallas kernels, packed_form(): pl.pallas_call(cycle_kernel, grid=(n_k,), out_shape=[jax.ShapeDtypeStruct...  9.58 us
    ppermute x3, waiting for transfers between devices, packed_form(): lax.ppermute(terms[d], 'blk', ring_y(RING - d))  7.79 us
    ppermute x3, starting transfers between devices, packed_form(): lax.ppermute(parts[d], 'red', ring_z(d))  6.57 us
    pallas_call x1, Pallas kernels, packed_form(): pl.pallas_call(unpack_kernel, grid=(n_k,), out_shape=jax.ShapeDtypeStruct...  6.33 us
    ppermute x3, starting transfers between devices, packed_form(): pb_y = [pb[0]] + [lax.ppermute(pb[d], 'blk', ring_y(d)) for d in (1, 3, 2)]  5.98 us
    ppermute x3, starting transfers between devices, packed_form(): across = [mine] + [lax.ppermute(mine, 'blk', ring_x(d)) for d in (1, 2, 3)]  5.72 us
  transfers between devices with their start and end apart: 19, of which 10 were waited for; matrix products, arithmetic and copies ran while one was open for 0% of the time, Pallas kernels for 5%

profile of v1, /device:TPU:0, one launch (start us, length us, event | category | flops | bytes accessed | tf_op | source)
XLA Modules:
  0.0 124.8 jit_solution(14390181974422196225)
XLA Ops:
  6.5 1.4 %ranks.1 = (s32[1,1024]{1,0:T(1,128)S(1)}, s32[1,1024]{1,0:T(1,128)S(1)}, s32[1]{0:T(128)}) custom-call(s32[1,1024]{1,0:T(1,128)} %bitcast.55), custom_call_target="tpu_custom_call" | custom-call | tf_op jit(solution)/shard_map/ranks/pallas_call | solution.py:378
  8.6 108.1 %conditional.1 = (f32[8,8,32,256]{3,2,1,0:T(8,128)S(1)}) conditional(s32[]{:T(128)} %bitcast.25, (s32[8]{0:T(128)}, s32[200]{0:T(256)}, s32[8]{0:T(128)}, s32[1024]{0:T(1024)}, bf16[8,8,32,256]{3,2,1,0:T(8,128)(2,1)}, /*index=5*/(), s32[4]{0:T(128)}, bf16[4,8,32,1024]{3,2,1,0:T(8,128)(2,1)}, (), bf16[4,8,32,1024]{3,2,1,0:T(8,128)(2,1)}, ...), branch_computations={%region_0.7_spmd, %region_7.8_spmd} | conditional | flops 17189898240 | bytes 311800608 | solution.py:536
  8.8 0.0 copy-start.8
  8.8 0.0 copy-start.9
  8.8 0.0 copy-start.11
  8.8 0.0 copy-start.15
  8.8 5.4 %pack.1 = (bf16[4,12,32,128]{3,2,1,0:T(8,128)(2,1)S(1)}, bf16[4,32,512]{2,1,0:T(8,128)(2,1)S(1)}, bf16[4,32,512]{2,1,0:T(8,128)(2,1)S(1)}, bf16[4,32,512]{2,1,0:T(8,128)(2,1)S(1)}, bf16[4,32,512]{2,1,0:T(8,128)(2,1)S(1)}) custom-call(s32[200]{0:T(256)} %get-tuple-element.68.occ_ref, s32[8]{0:T(128)} %get-tuple-element.69.si_ref, s32[8]{0:T(128)} %get-tuple-element.70.sj_ref, ...), custom_call_target="tpu_custom_call" | custom-call | flops 1073741824 | bytes 5242880 | tf_op jit(solution)/shard_map/cond/branch_1_fun/pack/pallas_call | solution.py:439
  14.2 1.7 %collective-permute-start.3 = (bf16[4,32,512]{2,1,0:T(8,128)(2,1)S(1)}, bf16[4,32,512]{2,1,0:T(8,128)(2,1)S(1)}, u32[]{:S(2)}, u32[]{:S(2)}) collective-permute-start(bf16[4,32,512]{2,1,0:T(8,128)(2,1)S(1)} %get-tuple-element.81), channel_id=1, source_target_pairs={{0,8},{4,12},{8,16},{12,20},{16,24},{20,28},{24,0},{28,4},{32,40},... | collective-permute-start | bytes 393224 | tf_op jit(solution)/shard_map/cond/branch_1_fun/ppermute | solution.py:462
  16.0 2.9 %collective-permute-start.4 = (bf16[4,32,512]{2,1,0:T(8,128)(2,1)S(1)}, bf16[4,32,512]{2,1,0:T(8,128)(2,1)S(1)}, u32[]{:S(2)}, u32[]{:S(2)}) collective-permute-start(bf16[4,32,512]{2,1,0:T(8,128)(2,1)S(1)} %get-tuple-element.82), channel_id=1, source_target_pairs={{0,16},{4,20},{8,24},{12,28},{16,0},{20,4},{24,8},{28,12},{32,48},... | collective-permute-start | bytes 393224 | tf_op jit(solution)/shard_map/cond/branch_1_fun/ppermute | solution.py:462
  18.9 1.3 %collective-permute-start.5 = (bf16[4,32,512]{2,1,0:T(8,128)(2,1)S(1)}, bf16[4,32,512]{2,1,0:T(8,128)(2,1)S(1)}, u32[]{:S(2)}, u32[]{:S(2)}) collective-permute-start(bf16[4,32,512]{2,1,0:T(8,128)(2,1)S(1)} %get-tuple-element.83), channel_id=1, source_target_pairs={{0,24},{4,28},{8,0},{12,4},{16,8},{20,12},{24,16},{28,20},{32,56},... | collective-permute-start | bytes 393224 | tf_op jit(solution)/shard_map/cond/branch_1_fun/ppermute | solution.py:462
  20.2 0.7 collective-permute-done.3
  20.9 4.0 %collective-permute-done.4 = bf16[4,32,512]{2,1,0:T(8,128)(2,1)S(1)} collective-permute-done((bf16[4,32,512]{2,1,0:T(8,128)(2,1)S(1)}, bf16[4,32,512]{2,1,0:T(8,128)(2,1)S(1)}, u32[]{:S(2)}, u32[]{:S(2)}) %collective-permute-start.4) | collective-permute-done | bytes 131104 | tf_op jit(solution)/shard_map/cond/branch_1_fun/ppermute | solution.py:462
  24.9 0.0 collective-permute-done.5
  24.9 0.1 pad_maximum_fusion.b0
  24.9 1.6 %collective-permute-start.6 = (bf16[4,4,32,512]{3,2,1,0:T(8,128)(2,1)S(1)}, bf16[4,4,32,512]{3,2,1,0:T(8,128)(2,1)S(1)}, u32[]{:S(2)}, u32[]{:S(2)}) collective-permute-start(bf16[4,4,32,512]{3,2,1,0:T(8,128)(2,1)S(1)} %pad_maximum_fusion.b0), channel_id=1, source_target_pairs={{0,32},{4,36},{8,40},{12,44},{16,48},{20,52},{24,56},{28,60},{32,6... | collective-permute-start | bytes 1572872 | tf_op jit(solution)/shard_map/cond/branch_1_fun/ppermute | solution.py:466
  26.5 2.7 %collective-permute-start.7 = (bf16[4,4,32,512]{3,2,1,0:T(8,128)(2,1)S(1)}, bf16[4,4,32,512]{3,2,1,0:T(8,128)(2,1)S(1)}, u32[]{:S(2)}, u32[]{:S(2)}) collective-permute-start(bf16[4,4,32,512]{3,2,1,0:T(8,128)(2,1)S(1)} %pad_maximum_fusion.b0), channel_id=1, source_target_pairs={{0,64},{4,68},{8,72},{12,76},{16,80},{20,84},{24,88},{28,92},{32,9... | collective-permute-start | bytes 1572872 | tf_op jit(solution)/shard_map/cond/branch_1_fun/ppermute | solution.py:466
  29.2 1.4 %collective-permute-start.8 = (bf16[4,4,32,512]{3,2,1,0:T(8,128)(2,1)S(1)}, bf16[4,4,32,512]{3,2,1,0:T(8,128)(2,1)S(1)}, u32[]{:S(2)}, u32[]{:S(2)}) collective-permute-start(bf16[4,4,32,512]{3,2,1,0:T(8,128)(2,1)S(1)} %pad_maximum_fusion.b0), channel_id=1, source_target_pairs={{0,96},{4,100},{8,104},{12,108},{16,112},{20,116},{24,120},{28,124... | collective-permute-start | bytes 1572872 | tf_op jit(solution)/shard_map/cond/branch_1_fun/ppermute | solution.py:466
  30.7 1.2 collective-permute-start
  31.9 2.4 %collective-permute-start.1 = (bf16[4,12,32,128]{3,2,1,0:T(8,128)(2,1)S(1)}, bf16[4,12,32,128]{3,2,1,0:T(8,128)(2,1)S(1)}, u32[]{:S(2)}, u32[]{:S(2)}) collective-permute-start(bf16[4,12,32,128]{3,2,1,0:T(8,128)(2,1)S(1)} %get-tuple-element.79.p0), channel_id=1, source_target_pairs={{0,16},{4,20},{8,24},{12,28},{16,0},{20,4},{24,8},{28,12},{32,48},... | collective-permute-start | bytes 1179656 | tf_op jit(solution)/shard_map/cond/branch_1_fun/ppermute | solution.py:465
  34.3 8.7 %collective-permute-done.p1 = bf16[4,12,32,128]{3,2,1,0:T(8,128)(2,1)S(1)} collective-permute-done((bf16[4,12,32,128]{3,2,1,0:T(8,128)(2,1)S(1)}, bf16[4,12,32,128]{3,2,1,0:T(8,128)(2,1)S(1)}, u32[]{:S(2)}, u32[]{:S(2)}) %collective-permute-start) | collective-permute-done | bytes 393248 | tf_op jit(solution)/shard_map/cond/branch_1_fun/ppermute | solution.py:465
  43.0 1.9 %collective-permute-start.2 = (bf16[4,12,32,128]{3,2,1,0:T(8,128)(2,1)S(1)}, bf16[4,12,32,128]{3,2,1,0:T(8,128)(2,1)S(1)}, u32[]{:S(2)}, u32[]{:S(2)}) collective-permute-start(bf16[4,12,32,128]{3,2,1,0:T(8,128)(2,1)S(1)} %get-tuple-element.79.p0), channel_id=1, source_target_pairs={{0,24},{4,28},{8,0},{12,4},{16,8},{20,12},{24,16},{28,20},{32,56},... | collective-permute-start | bytes 1179656 | tf_op jit(solution)/shard_map/cond/branch_1_fun/ppermute | solution.py:465
  44.9 5.2 %collective-permute-done.1.p2 = bf16[4,12,32,128]{3,2,1,0:T(8,128)(2,1)S(1)} collective-permute-done((bf16[4,12,32,128]{3,2,1,0:T(8,128)(2,1)S(1)}, bf16[4,12,32,128]{3,2,1,0:T(8,128)(2,1)S(1)}, u32[]{:S(2)}, u32[]{:S(2)}) %collective-permute-start.1) | collective-permute-done | bytes 393248 | tf_op jit(solution)/shard_map/cond/branch_1_fun/ppermute | solution.py:465
  50.1 0.0 collective-permute-start.9
  50.1 0.0 collective-permute-done.6.b1
  50.1 0.5 collective-permute-start.10
  50.6 0.6 collective-permute-done.7.b2
  51.2 0.0 collective-permute-start.11
  51.2 0.0 collective-permute-done.8.b3
  51.2 0.5 collective-permute-start.12
  51.8 0.0 collective-permute-done.2.p3
  51.8 0.0 copy-done.11
  51.8 0.0 copy-done.15
  51.8 6.3 %unpack.1.a_ref = bf16[4,1024,1024]{2,1,0:T(8,128)(2,1)} custom-call(s32[200]{0:T(256)S(1)} %copy-done.9, s32[8]{0:T(128)S(1)} %copy-done.11, s32[4]{0:T(128)S(1)} %copy-done.15, s32[1,1024]{1,0:T(1,128)S(1)} %bitcast.57, s32[1,1024]{1,0:T(1,128)S(1)} %get-tuple-element.76.rank_ref, bf16[4,12,32,128]{3,2,1,0:T(8,128)(2,1)S(1)} %get-tuple-element.79.p0, ...), custom_call_target="tpu_custom_call" | custom-call | flops 2147483648 | bytes 10485760 | tf_op jit(solution)/shard_map/cond/branch_1_fun/unpack/pallas_call | solution.py:470
  58.1 0.0 collective-permute-done.9.b4
  58.1 0.0 collective-permute-done.10.b5
  58.1 0.0 collective-permute-done.11.b6
  58.1 0.0 collective-permute-done.12.b7
  58.1 0.0 copy-start.19
  58.2 0.8 copy-done.19
  58.9 9.6 %cycle.1 = (f32[1024,128]{1,0:T(8,128)S(1)}, f32[1024,128]{1,0:T(8,128)S(1)}, f32[1024,128]{1,0:T(8,128)S(1)}, f32[1024,128]{1,0:T(8,128)S(1)}) custom-call(bf16[4,1024,1024]{2,1,0:T(8,128)(2,1)} %unpack.1.a_ref, bf16[4,4,32,512]{3,2,1,0:T(8,128)(2,1)S(1)} %pad_maximum_fusion.b0, bf16[4,4,32,512]{3,2,1,0:T(8,128)(2,1)S(1)} %collective-permute-done.6.b1, ...), custom_call_target="tpu_custom_call" | custom-call | flops 4294967296 | bytes 14680064 | tf_op jit(solution)/shard_map/cond/branch_1_fun/cycle/pallas_call | solution.py:489
  68.5 0.0 copy-start
  68.5 0.8 copy-done
  69.3 2.0 %collective-permute-start.13 = (f32[1024,128]{1,0:T(8,128)S(1)}, f32[1024,128]{1,0:T(8,128)S(1)}, u32[]{:S(2)}, u32[]{:S(2)}) collective-permute-start(f32[1024,128]{1,0:T(8,128)S(1)} %get-tuple-element.85), channel_id=1, source_target_pairs={{0,1},{1,2},{2,3},{3,0},{4,5},{5,6},{6,7},{7,4},{8,9},{9,10},{10,1... | collective-permute-start | bytes 1572872 | tf_op jit(solution)/shard_map/cond/branch_1_fun/ppermute | solution.py:502
  71.3 3.6 %collective-permute-start.14 = (f32[1024,128]{1,0:T(8,128)S(1)}, f32[1024,128]{1,0:T(8,128)S(1)}, u32[]{:S(2)}, u32[]{:S(2)}) collective-permute-start(f32[1024,128]{1,0:T(8,128)S(1)} %get-tuple-element.86), channel_id=1, source_target_pairs={{0,2},{1,3},{2,0},{3,1},{4,6},{5,7},{6,4},{7,5},{8,10},{9,11},{10,... | collective-permute-start | bytes 1572872 | tf_op jit(solution)/shard_map/cond/branch_1_fun/ppermute | solution.py:502
  74.9 1.0 collective-permute-start.15
  75.9 9.7 %collective-permute-done.13.o1 = f32[1024,128]{1,0:T(8,128)S(1)} collective-permute-done((f32[1024,128]{1,0:T(8,128)S(1)}, f32[1024,128]{1,0:T(8,128)S(1)}, u32[]{:S(2)}, u32[]{:S(2)}) %collective-permute-start.13) | collective-permute-done | bytes 524320 | tf_op jit(solution)/shard_map/cond/branch_1_fun/ppermute | solution.py:502
  85.6 12.4 %collective-permute-done.14.o2 = f32[1024,128]{1,0:T(8,128)S(1)} collective-permute-done((f32[1024,128]{1,0:T(8,128)S(1)}, f32[1024,128]{1,0:T(8,128)S(1)}, u32[]{:S(2)}, u32[]{:S(2)}) %collective-permute-start.14) | collective-permute-done | bytes 524320 | tf_op jit(solution)/shard_map/cond/branch_1_fun/ppermute | solution.py:502
  98.0 0.0 collective-permute-done.15.o3
  98.0 0.0 copy-done.5
  98.0 0.8 copy-done.6
  98.8 0.2 copy-done.7
  99.0 2.3 %sums.1 = (f32[8,32,128]{2,1,0:T(8,128)}, f32[8,32,128]{2,1,0:T(8,128)}, f32[8,32,128]{2,1,0:T(8,128)}, f32[8,32,128]{2,1,0:T(8,128)}) custom-call(f32[1024,128]{1,0:T(8,128)} %copy-done, f32[1024,128]{1,0:T(8,128)} %copy-done.5, f32[1024,128]{1,0:T(8,128)} %copy-done.6, f32[1024,128]{1,0:T(8,128)} %copy-done.7), custom_call_target="tpu_custom_call" | custom-call | flops 524288 | bytes 3145728 | tf_op jit(solution)/shard_map/cond/branch_1_fun/sums/pallas_call | solution.py:503
  101.3 2.4 %collective-permute-start.16 = (f32[8,32,128]{2,1,0:T(8,128)}, f32[8,32,128]{2,1,0:T(8,128)S(1)}, u32[]{:S(2)}, u32[]{:S(2)}) collective-permute-start(f32[8,32,128]{2,1,0:T(8,128)} %get-tuple-element.89), channel_id=1, source_target_pairs={{0,24},{4,28},{8,0},{12,4},{16,8},{20,12},{24,16},{28,20},{32,56},... | collective-permute-start | bytes 393224 | tf_op jit(solution)/shard_map/cond/branch_1_fun/ppermute | solution.py:511
  103.8 0.9 collective-permute-start.17
  104.7 0.1 collective-permute-start.18
  104.8 4.2 %collective-permute-done.16.t1 = f32[8,32,128]{2,1,0:T(8,128)S(1)} collective-permute-done((f32[8,32,128]{2,1,0:T(8,128)}, f32[8,32,128]{2,1,0:T(8,128)S(1)}, u32[]{:S(2)}, u32[]{:S(2)}) %collective-permute-start.16) | collective-permute-done | bytes 131104 | tf_op jit(solution)/shard_map/cond/branch_1_fun/ppermute | solution.py:511
  109.0 2.2 %collective-permute-done.17.t2 = f32[8,32,128]{2,1,0:T(8,128)S(1)} collective-permute-done((f32[8,32,128]{2,1,0:T(8,128)}, f32[8,32,128]{2,1,0:T(8,128)S(1)}, u32[]{:S(2)}, u32[]{:S(2)}) %collective-permute-start.17) | collective-permute-done | bytes 131104 | tf_op jit(solution)/shard_map/cond/branch_1_fun/ppermute | solution.py:511
  111.2 1.3 %collective-permute-done.18.t3 = f32[8,32,128]{2,1,0:T(8,128)S(1)} collective-permute-done((f32[8,32,128]{2,1,0:T(8,128)}, f32[8,32,128]{2,1,0:T(8,128)S(1)}, u32[]{:S(2)}, u32[]{:S(2)}) %collective-permute-start.18) | collective-permute-done | bytes 131104 | tf_op jit(solution)/shard_map/cond/branch_1_fun/ppermute | solution.py:511
  112.6 0.0 copy-done.3
  112.6 0.0 copy-done.14
  112.6 0.9 copy-done.1
  113.5 3.1 %update.1 = f32[8,8,32,256]{3,2,1,0:T(8,128)S(1)} custom-call(s32[200]{0:T(256)S(1)} %copy-done.9, s32[8]{0:T(128)S(1)} %copy-done.11, s32[8]{0:T(128)S(1)} %copy-done.13, f32[200]{0:T(256)S(1)} %copy-done.17, s32[1,1024]{1,0:T(1,128)S(1)} %bitcast.58, f32[1,1024]{1,0:T(1,128)S(1)} %bitcast.59, s32[1,1024]{1,0:T(1,128)S(1)} %get-tuple-element.74.part_ref, ...), custom_call_target="tpu_custom_call" | custom-call | flops 402653184 | bytes 4194304 | tf_op jit(solution)/shard_map/cond/branch_1_fun/update/pallas_call | solution.py:513
  116.6 0.0 copy-start.4
  116.6 1.3 %copy-done.4 = f32[8,8,32,256]{3,2,1,0:T(8,128)} copy-done((f32[8,8,32,256]{3,2,1,0:T(8,128)}, f32[8,8,32,256]{3,2,1,0:T(8,128)S(1)}, u32[]{:S(2)}) %copy-start.4) | copy-done | bytes 2097176
  (12 shorter events, 0.0 us)
Async XLA Ops:
  8.8 43.0 %copy-start.8 = (s32[1024]{0:T(1024)S(1)}, s32[1024]{0:T(1024)}, u32[]{:S(2)}) copy-start(s32[1024]{0:T(1024)} %get-tuple-element.72) | copy-start | bytes 12292 | tf_op jit(solution)/shard_map/cond
  8.8 43.0 %copy-start.9 = (s32[200]{0:T(256)S(1)}, s32[200]{0:T(256)}, u32[]{:S(2)}) copy-start(s32[200]{0:T(256)} %get-tuple-element.68.occ_ref) | copy-start | bytes 2404 | tf_op jit(solution)/shard_map/cond
  8.8 43.0 %copy-start.11 = (s32[8]{0:T(128)S(1)}, s32[8]{0:T(128)}, u32[]{:S(2)}) copy-start(s32[8]{0:T(128)} %get-tuple-element.69.si_ref) | copy-start | bytes 100 | tf_op jit(solution)/shard_map/cond
  8.8 43.0 %copy-start.15 = (s32[4]{0:T(128)S(1)}, s32[4]{0:T(128)}, u32[]{:S(2)}) copy-start(s32[4]{0:T(128)} %get-tuple-element.75.sk_ref) | copy-start | bytes 52 | tf_op jit(solution)/shard_map/cond
  14.2 6.7 %collective-permute-start.3 = (bf16[4,32,512]{2,1,0:T(8,128)(2,1)S(1)}, bf16[4,32,512]{2,1,0:T(8,128)(2,1)S(1)}, u32[]{:S(2)}, u32[]{:S(2)}) collective-permute-start(bf16[4,32,512]{2,1,0:T(8,128)(2,1)S(1)} %get-tuple-element.81), channel_id=1, source_target_pairs={{0,8},{4,12},{8,16},{12,20},{16,24},{20,28},{24,0},{28,4},{32,40},... | collective-permute-start | bytes 393224 | tf_op jit(solution)/shard_map/cond/branch_1_fun/ppermute | solution.py:462
  16.0 8.9 %collective-permute-start.4 = (bf16[4,32,512]{2,1,0:T(8,128)(2,1)S(1)}, bf16[4,32,512]{2,1,0:T(8,128)(2,1)S(1)}, u32[]{:S(2)}, u32[]{:S(2)}) collective-permute-start(bf16[4,32,512]{2,1,0:T(8,128)(2,1)S(1)} %get-tuple-element.82), channel_id=1, source_target_pairs={{0,16},{4,20},{8,24},{12,28},{16,0},{20,4},{24,8},{28,12},{32,48},... | collective-permute-start | bytes 393224 | tf_op jit(solution)/shard_map/cond/branch_1_fun/ppermute | solution.py:462
  18.9 6.0 %collective-permute-start.5 = (bf16[4,32,512]{2,1,0:T(8,128)(2,1)S(1)}, bf16[4,32,512]{2,1,0:T(8,128)(2,1)S(1)}, u32[]{:S(2)}, u32[]{:S(2)}) collective-permute-start(bf16[4,32,512]{2,1,0:T(8,128)(2,1)S(1)} %get-tuple-element.83), channel_id=1, source_target_pairs={{0,24},{4,28},{8,0},{12,4},{16,8},{20,12},{24,16},{28,20},{32,56},... | collective-permute-start | bytes 393224 | tf_op jit(solution)/shard_map/cond/branch_1_fun/ppermute | solution.py:462
  24.9 25.2 %collective-permute-start.6 = (bf16[4,4,32,512]{3,2,1,0:T(8,128)(2,1)S(1)}, bf16[4,4,32,512]{3,2,1,0:T(8,128)(2,1)S(1)}, u32[]{:S(2)}, u32[]{:S(2)}) collective-permute-start(bf16[4,4,32,512]{3,2,1,0:T(8,128)(2,1)S(1)} %pad_maximum_fusion.b0), channel_id=1, source_target_pairs={{0,32},{4,36},{8,40},{12,44},{16,48},{20,52},{24,56},{28,60},{32,6... | collective-permute-start | bytes 1572872 | tf_op jit(solution)/shard_map/cond/branch_1_fun/ppermute | solution.py:466
  26.5 24.7 %collective-permute-start.7 = (bf16[4,4,32,512]{3,2,1,0:T(8,128)(2,1)S(1)}, bf16[4,4,32,512]{3,2,1,0:T(8,128)(2,1)S(1)}, u32[]{:S(2)}, u32[]{:S(2)}) collective-permute-start(bf16[4,4,32,512]{3,2,1,0:T(8,128)(2,1)S(1)} %pad_maximum_fusion.b0), channel_id=1, source_target_pairs={{0,64},{4,68},{8,72},{12,76},{16,80},{20,84},{24,88},{28,92},{32,9... | collective-permute-start | bytes 1572872 | tf_op jit(solution)/shard_map/cond/branch_1_fun/ppermute | solution.py:466
  29.2 22.0 %collective-permute-start.8 = (bf16[4,4,32,512]{3,2,1,0:T(8,128)(2,1)S(1)}, bf16[4,4,32,512]{3,2,1,0:T(8,128)(2,1)S(1)}, u32[]{:S(2)}, u32[]{:S(2)}) collective-permute-start(bf16[4,4,32,512]{3,2,1,0:T(8,128)(2,1)S(1)} %pad_maximum_fusion.b0), channel_id=1, source_target_pairs={{0,96},{4,100},{8,104},{12,108},{16,112},{20,116},{24,120},{28,124... | collective-permute-start | bytes 1572872 | tf_op jit(solution)/shard_map/cond/branch_1_fun/ppermute | solution.py:466
  30.7 12.3 %collective-permute-start = (bf16[4,12,32,128]{3,2,1,0:T(8,128)(2,1)S(1)}, bf16[4,12,32,128]{3,2,1,0:T(8,128)(2,1)S(1)}, u32[]{:S(2)}, u32[]{:S(2)}) collective-permute-start(bf16[4,12,32,128]{3,2,1,0:T(8,128)(2,1)S(1)} %get-tuple-element.79.p0), channel_id=1, source_target_pairs={{0,8},{4,12},{8,16},{12,20},{16,24},{20,28},{24,0},{28,4},{32,40},... | collective-permute-start | bytes 1179656 | tf_op jit(solution)/shard_map/cond/branch_1_fun/ppermute | solution.py:465
  31.9 18.2 %collective-permute-start.1 = (bf16[4,12,32,128]{3,2,1,0:T(8,128)(2,1)S(1)}, bf16[4,12,32,128]{3,2,1,0:T(8,128)(2,1)S(1)}, u32[]{:S(2)}, u32[]{:S(2)}) collective-permute-start(bf16[4,12,32,128]{3,2,1,0:T(8,128)(2,1)S(1)} %get-tuple-element.79.p0), channel_id=1, source_target_pairs={{0,16},{4,20},{8,24},{12,28},{16,0},{20,4},{24,8},{28,12},{32,48},... | collective-permute-start | bytes 1179656 | tf_op jit(solution)/shard_map/cond/branch_1_fun/ppermute | solution.py:465
  43.0 8.8 %collective-permute-start.2 = (bf16[4,12,32,128]{3,2,1,0:T(8,128)(2,1)S(1)}, bf16[4,12,32,128]{3,2,1,0:T(8,128)(2,1)S(1)}, u32[]{:S(2)}, u32[]{:S(2)}) collective-permute-start(bf16[4,12,32,128]{3,2,1,0:T(8,128)(2,1)S(1)} %get-tuple-element.79.p0), channel_id=1, source_target_pairs={{0,24},{4,28},{8,0},{12,4},{16,8},{20,12},{24,16},{28,20},{32,56},... | collective-permute-start | bytes 1179656 | tf_op jit(solution)/shard_map/cond/branch_1_fun/ppermute | solution.py:465
  50.1 8.0 %collective-permute-start.9 = (bf16[4,4,32,512]{3,2,1,0:T(8,128)(2,1)S(1)}, bf16[4,4,32,512]{3,2,1,0:T(8,128)(2,1)S(1)}, u32[]{:S(2)}, u32[]{:S(2)}) collective-permute-start(bf16[4,4,32,512]{3,2,1,0:T(8,128)(2,1)S(1)} %pad_maximum_fusion.b0), channel_id=1, source_target_pairs={{0,4},{4,0},{8,12},{12,8},{16,20},{20,16},{24,28},{28,24},{32,36},... | collective-permute-start | bytes 1572872 | tf_op jit(solution)/shard_map/cond/branch_1_fun/ppermute | solution.py:467
  50.1 8.0 %collective-permute-start.10 = (bf16[4,4,32,512]{3,2,1,0:T(8,128)(2,1)S(1)}, bf16[4,4,32,512]{3,2,1,0:T(8,128)(2,1)S(1)}, u32[]{:S(2)}, u32[]{:S(2)}) collective-permute-start(bf16[4,4,32,512]{3,2,1,0:T(8,128)(2,1)S(1)} %collective-permute-done.6.b1), channel_id=1, source_target_pairs={{0,4},{4,0},{8,12},{12,8},{16,20},{20,16},{24,28},{28,24},{32,36},... | collective-permute-start | bytes 1572872 | tf_op jit(solution)/shard_map/cond/branch_1_fun/ppermute | solution.py:467
  51.2 6.9 %collective-permute-start.11 = (bf16[4,4,32,512]{3,2,1,0:T(8,128)(2,1)S(1)}, bf16[4,4,32,512]{3,2,1,0:T(8,128)(2,1)S(1)}, u32[]{:S(2)}, u32[]{:S(2)}) collective-permute-start(bf16[4,4,32,512]{3,2,1,0:T(8,128)(2,1)S(1)} %collective-permute-done.7.b2), channel_id=1, source_target_pairs={{0,4},{4,0},{8,12},{12,8},{16,20},{20,16},{24,28},{28,24},{32,36},... | collective-permute-start | bytes 1572872 | tf_op jit(solution)/shard_map/cond/branch_1_fun/ppermute | solution.py:467
  51.2 6.9 %collective-permute-start.12 = (bf16[4,4,32,512]{3,2,1,0:T(8,128)(2,1)S(1)}, bf16[4,4,32,512]{3,2,1,0:T(8,128)(2,1)S(1)}, u32[]{:S(2)}, u32[]{:S(2)}) collective-permute-start(bf16[4,4,32,512]{3,2,1,0:T(8,128)(2,1)S(1)} %collective-permute-done.8.b3), channel_id=1, source_target_pairs={{0,4},{4,0},{8,12},{12,8},{16,20},{20,16},{24,28},{28,24},{32,36},... | collective-permute-start | bytes 1572872 | tf_op jit(solution)/shard_map/cond/branch_1_fun/ppermute | solution.py:467
  58.1 0.8 copy-start.19
  68.5 0.8 copy-start
  69.3 43.2 %copy-start.3 = (bf16[8,8,32,256]{3,2,1,0:T(8,128)(2,1)S(1)}, bf16[8,8,32,256]{3,2,1,0:T(8,128)(2,1)}, u32[]{:S(2)}) copy-start(bf16[8,8,32,256]{3,2,1,0:T(8,128)(2,1)} %get-tuple-element.92.int_ref) | copy-start | bytes 3145732 | tf_op jit(solution)/shard_map/cond
  69.3 43.2 %copy-start.13 = (s32[8]{0:T(128)S(1)}, s32[8]{0:T(128)}, u32[]{:S(2)}) copy-start(s32[8]{0:T(128)} %get-tuple-element.70.sj_ref) | copy-start | bytes 100 | tf_op jit(solution)/shard_map/cond
  69.3 43.2 %copy-start.14 = (f32[1024]{0:T(1024)S(1)}, f32[1024]{0:T(1024)}, u32[]{:S(2)}) copy-start(f32[1024]{0:T(1024)} %get-tuple-element.73) | copy-start | bytes 12292 | tf_op jit(solution)/shard_map/cond
  69.3 43.2 %copy-start.17 = (f32[200]{0:T(256)S(1)}, f32[200]{0:T(256)}, u32[]{:S(2)}) copy-start(f32[200]{0:T(256)} %get-tuple-element.71.oe_ref) | copy-start | bytes 2404 | tf_op jit(solution)/shard_map/cond
  69.3 16.2 %collective-permute-start.13 = (f32[1024,128]{1,0:T(8,128)S(1)}, f32[1024,128]{1,0:T(8,128)S(1)}, u32[]{:S(2)}, u32[]{:S(2)}) collective-permute-start(f32[1024,128]{1,0:T(8,128)S(1)} %get-tuple-element.85), channel_id=1, source_target_pairs={{0,1},{1,2},{2,3},{3,0},{4,5},{5,6},{6,7},{7,4},{8,9},{9,10},{10,1... | collective-permute-start | bytes 1572872 | tf_op jit(solution)/shard_map/cond/branch_1_fun/ppermute | solution.py:502
  71.3 26.6 %collective-permute-start.14 = (f32[1024,128]{1,0:T(8,128)S(1)}, f32[1024,128]{1,0:T(8,128)S(1)}, u32[]{:S(2)}, u32[]{:S(2)}) collective-permute-start(f32[1024,128]{1,0:T(8,128)S(1)} %get-tuple-element.86), channel_id=1, source_target_pairs={{0,2},{1,3},{2,0},{3,1},{4,6},{5,7},{6,4},{7,5},{8,10},{9,11},{10,... | collective-permute-start | bytes 1572872 | tf_op jit(solution)/shard_map/cond/branch_1_fun/ppermute | solution.py:502
  74.9 23.1 %collective-permute-start.15 = (f32[1024,128]{1,0:T(8,128)S(1)}, f32[1024,128]{1,0:T(8,128)S(1)}, u32[]{:S(2)}, u32[]{:S(2)}) collective-permute-start(f32[1024,128]{1,0:T(8,128)S(1)} %get-tuple-element.87), channel_id=1, source_target_pairs={{0,3},{1,0},{2,1},{3,2},{4,7},{5,4},{6,5},{7,6},{8,11},{9,8},{10,9... | collective-permute-start | bytes 1572872 | tf_op jit(solution)/shard_map/cond/branch_1_fun/ppermute | solution.py:502
  85.6 12.4 %copy-start.5 = (f32[1024,128]{1,0:T(8,128)}, f32[1024,128]{1,0:T(8,128)S(1)}, u32[]{:S(2)}) copy-start(f32[1024,128]{1,0:T(8,128)S(1)} %collective-permute-done.13.o1) | copy-start | bytes 1572868 | tf_op jit(solution)/shard_map/cond
  98.0 0.8 copy-start.6
  98.0 1.0 copy-start.7
  101.3 7.6 %collective-permute-start.16 = (f32[8,32,128]{2,1,0:T(8,128)}, f32[8,32,128]{2,1,0:T(8,128)S(1)}, u32[]{:S(2)}, u32[]{:S(2)}) collective-permute-start(f32[8,32,128]{2,1,0:T(8,128)} %get-tuple-element.89), channel_id=1, source_target_pairs={{0,24},{4,28},{8,0},{12,4},{16,8},{20,12},{24,16},{28,20},{32,56},... | collective-permute-start | bytes 393224 | tf_op jit(solution)/shard_map/cond/branch_1_fun/ppermute | solution.py:511
  103.8 7.4 %collective-permute-start.17 = (f32[8,32,128]{2,1,0:T(8,128)}, f32[8,32,128]{2,1,0:T(8,128)S(1)}, u32[]{:S(2)}, u32[]{:S(2)}) collective-permute-start(f32[8,32,128]{2,1,0:T(8,128)} %get-tuple-element.90), channel_id=1, source_target_pairs={{0,16},{4,20},{8,24},{12,28},{16,0},{20,4},{24,8},{28,12},{32,48},... | collective-permute-start | bytes 393224 | tf_op jit(solution)/shard_map/cond/branch_1_fun/ppermute | solution.py:511
  104.7 7.8 %collective-permute-start.18 = (f32[8,32,128]{2,1,0:T(8,128)}, f32[8,32,128]{2,1,0:T(8,128)S(1)}, u32[]{:S(2)}, u32[]{:S(2)}) collective-permute-start(f32[8,32,128]{2,1,0:T(8,128)} %get-tuple-element.91), channel_id=1, source_target_pairs={{0,8},{4,12},{8,16},{12,20},{16,24},{20,28},{24,0},{28,4},{32,40},... | collective-permute-start | bytes 393224 | tf_op jit(solution)/shard_map/cond/branch_1_fun/ppermute | solution.py:511
  112.6 0.9 copy-start.1
  116.6 1.3 %copy-start.4 = (f32[8,8,32,256]{3,2,1,0:T(8,128)}, f32[8,8,32,256]{3,2,1,0:T(8,128)S(1)}, u32[]{:S(2)}) copy-start(f32[8,8,32,256]{3,2,1,0:T(8,128)S(1)} %get-tuple-element.153) | copy-start | bytes 6291460

commit v2 on v1

--- a/solution.py
+++ b/solution.py
@@ -17,6 +17,8 @@
 WIDE = 192
 PART = 64
 NT = (((1,), (1,)), ((), ()))
+STEPS = ((2, 1), (3, 0))
+CHUNKS = 2
 
 
 def table_lookup(table, picks):
@@ -74,8 +76,8 @@
     partial_cycle = jnp.einsum(
         "kiac,kjcb->ijab", amp_owner, dre_owner, preferred_element_type=jnp.float32
     )
-    summed = lax.psum_scatter(partial_cycle, "red", scatter_dimension=3, tiled=True)
-    cycle_pairs = summed.reshape(pair_count, virt_all, cols_kept)
+    by_cols = partial_cycle.reshape(pair_count, virt_all, red_size, cols_kept)
+    cycle_pairs = lax.all_to_all(by_cols, "red", split_axis=2, concat_axis=2, tiled=True).sum(axis=2)
     cycle_kept = lax.all_to_all(
         cycle_pairs, "blk", split_axis=1, concat_axis=0, tiled=True
     ).reshape(slab_rows, occ_cols, virt_rows, cols_kept)
@@ -112,6 +114,12 @@
     hit = iota((count, wide), 1) == iota((count, wide), 0) + first
     kept = jnp.where(hit, jnp.broadcast_to(row.astype(F32), (count, wide)), 0.0)
     return jnp.sum(kept, axis=1, keepdims=True).astype(row.dtype)
+
+
+def one_hot(count, first, row):
+    slot = (iota((count, 1), 0) + first).astype(F32).astype(BF16)
+    there = jnp.clip(row, -1, 256).astype(F32).astype(BF16)
+    return jnp.where(slot == there, jnp.ones((), BF16), jnp.zeros((), BF16))
 
 
 def rank_kernel(lv_ref, rank_ref, part_ref, fits_ref):
@@ -133,85 +141,84 @@
     fits_ref[0] = fits.astype(I32)
 
 
-def pack_kernel(
-    occ_ref,
-    si_ref,
-    sj_ref,
-    sk_ref,
-    lv_ref,
-    rank_ref,
-    part_ref,
-    amp_ref,
-    dre_ref,
-    pa_ref,
-    pb0_ref,
-    pb1_ref,
-    pb2_ref,
-    pb3_ref,
-    hot_main,
-    hot_low,
-    hot_high,
-    hot_part,
-    own_label,
-    kept,
+def masked_rows(kept, at, label, own_label, lv, block):
+    rows = block.shape[0]
+    wanted = jnp.bitwise_xor(own_label, label).astype(F32).astype(BF16)
+    kept[at * rows : (at + 1) * rows, :] = jnp.where(wanted == lv, block, jnp.zeros((), BF16))
+
+
+def pack_dressed_kernel(
+    occ_ref, sj_ref, sk_ref, lv_ref, part_ref, dre_ref, p0, p1, p2, p3, hot_part, own_label, kept
 ):
     _, y, _, z = coords()
     k = pl.program_id(0)
-    rows, wide = amp_ref.shape[2:]
+    rows, wide = dre_ref.shape[2:]
+
+    @pl.when(k == 0)
+    def _():
+        step = (iota((1, wide), 1) // (wide // RING) - z + RING) % RING
+        hot_part[...] = one_hot(RING * PART, 0, step * PART + jnp.minimum(part_ref[...], PART - 1))
+        own_label[...] = picked_column(lv_ref[...], lax.axis_index("blk") * rows, rows)
+
+    lk = occ_ref[sk_ref[k]]
+    lv = lv_ref[...].astype(F32).astype(BF16)
+    for d in range(RING):
+        for jj in range(CORES):
+            j = ((y + d) % RING) * CORES + jj
+            label = jnp.bitwise_xor(lk, occ_ref[sj_ref[j]])
+            masked_rows(kept, jj * RING + d, label, own_label[...], lv, dre_ref[0, j])
+    packed = lax.dot_general(kept[...], hot_part[...], NT, preferred_element_type=F32)
+    for d, out in enumerate((p0, p1, p2, p3)):
+        even = packed[d * rows : (d + 1) * rows]
+        odd = packed[(RING + d) * rows : (RING + d + 1) * rows]
+        for chunk, steps in enumerate(STEPS):
+            pieces = []
+            for s in steps:
+                pieces += [even[:, s * PART : (s + 1) * PART], odd[:, s * PART : (s + 1) * PART]]
+            out[chunk, 0] = jnp.concatenate(pieces, axis=1).astype(BF16)
+
+
+def pack_amplitudes_kernel(
+    occ_ref, si_ref, sk_ref, lv_ref, rank_ref, amp_ref, pa_ref, hot_main, hot_low, hot_high, own_label, kept
+):
+    k = pl.program_id(0)
+    n_i, rows, wide = amp_ref.shape[1:]
     half = hot_main.shape[0]
 
     @pl.when(k == 0)
     def _():
         rank = rank_ref[...]
-        slot = iota((half, wide), 0)
-        hot_main[...] = (slot == rank).astype(F32).astype(BF16)
-        hot_low[...] = jnp.logical_and(slot + half == rank, slot < PART).astype(F32).astype(BF16)
-        hot_high[...] = (
-            jnp.logical_and(slot + half - PART == rank, slot >= PART).astype(F32).astype(BF16)
-        )
-        step = (iota((1, wide), 1) // (wide // RING) - z + RING) % RING
-        hot_part[...] = (
-            (iota((RING * PART, wide), 0) == step * PART + part_ref[...]).astype(F32).astype(BF16)
-        )
+        tail = one_hot(half - PART, half, rank)
+        empty = jnp.zeros((PART, wide), BF16)
+        hot_main[...] = one_hot(half, 0, rank)
+        hot_low[:PART] = tail
+        hot_low[PART:] = empty
+        hot_high[:PART] = empty
+        hot_high[PART:] = tail
         own_label[...] = picked_column(lv_ref[...], lax.axis_index("blk") * rows, rows)
 
-    lv = lv_ref[...]
     lk = occ_ref[sk_ref[k]]
-
-    def put(at, label, block):
-        keep = jnp.bitwise_xor(own_label[...], jnp.bitwise_xor(lk, label)) == lv
-        kept[at * rows : (at + 1) * rows, :] = jnp.where(keep, block.astype(F32), 0.0).astype(BF16)
-
-    n_i = amp_ref.shape[1]
+    lv = lv_ref[...].astype(F32).astype(BF16)
     for i in range(n_i):
-        put(i, occ_ref[si_ref[i]], amp_ref[0, i])
+        label = jnp.bitwise_xor(lk, occ_ref[si_ref[i]])
+        masked_rows(kept, i, label, own_label[...], lv, amp_ref[0, i])
     main = lax.dot_general(kept[...], hot_main[...], NT, preferred_element_type=F32)
-    pa_ref[0, :n_i] = main.astype(BF16).reshape(n_i, rows, half)
+    main = main.astype(BF16).reshape(n_i, rows, half)
     lower = n_i * rows // 2
     rest = lax.dot_general(kept[:lower], hot_low[...], NT, preferred_element_type=F32)
     rest += lax.dot_general(kept[lower:], hot_high[...], NT, preferred_element_type=F32)
-    pa_ref[0, n_i:] = rest.astype(BF16).reshape(n_i // 2, rows, half)
-
+    rest = rest.astype(BF16).reshape(n_i // 2, rows, half)
     for d in range(RING):
-        for jj in range(CORES):
-            j = ((y + d) % RING) * CORES + jj
-            put(jj * RING + d, occ_ref[sj_ref[j]], dre_ref[0, j])
-    packed = lax.dot_general(kept[...], hot_part[...], NT, preferred_element_type=F32)
-    for d, out in enumerate((pb0_ref, pb1_ref, pb2_ref, pb3_ref)):
-        even = packed[d * rows : (d + 1) * rows]
-        odd = packed[(RING + d) * rows : (RING + d + 1) * rows]
-        pieces = []
-        for s in range(RING):
-            pieces += [even[:, s * PART : (s + 1) * PART], odd[:, s * PART : (s + 1) * PART]]
-        out[0] = jnp.concatenate(pieces, axis=1).astype(BF16)
+        pa_ref[d, 0, :n_i] = main
+        pa_ref[d, 0, n_i:] = rest
 
 
 def unpack_kernel(
-    occ_ref, si_ref, sk_ref, lv_ref, rank_ref, p0, p1, p2, p3, out_ref, hot_low, hot_high, order, labels
+    occ_ref, si_ref, sk_ref, lv_ref, rank_ref, pa_ref, out_ref, hot_low, hot_high, order, labels
 ):
     x, y, core, _ = coords()
     k = pl.program_id(0)
-    n_rest, rows, half = p0.shape[1:]
+    n_rest, rows, half = pa_ref.shape[2:]
     n_i = n_rest * 2 // 3
     wide = lv_ref.shape[1]
 
@@ -232,23 +239,25 @@
             jnp.broadcast_to(jnp.minimum(rank_ref[...], 255), (16, wide)),
         )
         moved = jnp.dot(both.astype(F32).astype(BF16), pick, preferred_element_type=F32).astype(I32)
-        order[...] = moved[0:1]
+        order[...] = moved[0:1].astype(F32).astype(BF16)
         rank = moved[1:2]
-        slot = iota((half, wide), 0)
-        main = (slot == rank).astype(F32).astype(BF16)
+        main = one_hot(half, 0, rank)
+        tail = one_hot(half - PART, half, rank)
+        empty = jnp.zeros((PART, wide), BF16)
         hot_low[:half] = main
         hot_high[:half] = main
-        hot_low[half:] = jnp.logical_and(slot + half == rank, slot < PART).astype(F32).astype(BF16)
-        hot_high[half:] = (
-            jnp.logical_and(slot + half - PART == rank, slot >= PART).astype(F32).astype(BF16)
-        )
+        hot_low[half : half + PART] = tail
+        hot_low[half + PART :] = empty
+        hot_high[half : half + PART] = empty
+        hot_high[half + PART :] = tail
         for d in range(RING):
             first = x * (rows * 8) + ((y - d + RING) % RING) * (rows * 2) + core * rows
             labels[d] = picked_column(lv_ref[...], first, rows)
 
     lk = occ_ref[sk_ref[k]]
     group = n_i // 2
-    for d, block in enumerate((p0, p1, p2, p3)):
+    for d in range(RING):
+        block = pa_ref.at[(y - d + RING) % RING]
         rest = block[0, n_i:].reshape(group * rows, half)
         for side, hot in enumerate((hot_low, hot_high)):
             main = block[0, side * group : (side + 1) * group].reshape(group * rows, half)
@@ -258,46 +267,41 @@
             for g in range(group):
                 i = side * group + g
                 label = jnp.bitwise_xor(lk, occ_ref[si_ref[i]])
-                keep = jnp.bitwise_xor(labels[d], label) == order[...]
+                wanted = jnp.bitwise_xor(labels[d], label).astype(F32).astype(BF16)
                 at = (d * n_i + i) * rows
                 out_ref[0, at : at + rows, :] = jnp.where(
-                    keep, spread[g * rows : (g + 1) * rows], 0.0
-                ).astype(BF16)
-
-
-def cycle_kernel(a_ref, b0, b1, b2, b3, b4, b5, b6, b7, o0, o1, o2, o3, b_all, total):
+                    wanted == order[...],
+                    spread[g * rows : (g + 1) * rows].astype(BF16),
+                    jnp.zeros((), BF16),
+                )
+
+
+def cycle_kernel(a_ref, b0, b1, b2, b3, b4, b5, b6, b7, o0, o1, b_all, total):
     k = pl.program_id(0)
     depth = b0.shape[0] * b0.shape[2]
     for n, b in enumerate((b0, b1, b2, b3, b4, b5, b6, b7)):
         b_all[n * depth : (n + 1) * depth, :] = b[:, 0].reshape(depth, b.shape[3])
-    rows = a_ref.shape[1]
-    step = rows // 4
+    term = jnp.dot(a_ref[0], b_all[...], preferred_element_type=F32)
     lanes = o0.shape[1]
-    for r in range(4):
-        at = slice(r * step, (r + 1) * step)
-        term = jnp.dot(a_ref[0, at], b_all[...], preferred_element_type=F32)
-
-        @pl.when(k == 0)
-        def _():
-            total[at] = term
-
-        @pl.when(jnp.logical_and(k > 0, k < pl.num_programs(0) - 1))
-        def _():
-            total[at] += term
-
-        @pl.when(k == pl.num_programs(0) - 1)
-        def _():
-            full = total[at] + term
-            for d, out in enumerate((o0, o1, o2, o3)):
-                out[at] = full[:, d * lanes : (d + 1) * lanes]
+
+    @pl.when(k == 0)
+    def _():
+        total[...] = term
+
+    @pl.when(jnp.logical_and(k > 0, k < pl.num_programs(0) - 1))
+    def _():
+        total[...] += term
+
+    @pl.when(k == pl.num_programs(0) - 1)
+    def _():
+        full = total[...] + term
+        for d, out in enumerate((o0, o1)):
+            out[...] = full[:, d * lanes : (d + 1) * lanes]
 
 
 def sum_kernel(o0, o1, o2, o3, s0, s1, s2, s3):
-    rows = s0.shape[0] * s0.shape[1]
     for d, out in enumerate((s0, s1, s2, s3)):
-        at = slice(d * rows, (d + 1) * rows)
-        full = ((o0[at] + o1[at]) + o2[at]) + o3[at]
-        out[...] = full.reshape(out.shape)
+        out[...] = ((o0[d] + o1[d]) + o2[d]) + o3[d]
 
 
 def update_kernel(
@@ -329,9 +333,9 @@
         slot = iota((lanes, kept), 0)
         part = part_ref[:, cols]
         for jj in range(CORES):
-            hot[:, jj * kept : (jj + 1) * kept] = (
-                (slot == part + jj * PART).astype(F32).astype(BF16)
-            )
+            one = (slot == part + jj * PART).astype(F32).astype(BF16)
+            for n in range(3):
+                hot[n * lanes : (n + 1) * lanes, jj * kept : (jj + 1) * kept] = one
         first = lax.axis_index("blk") * rows
         own_label[...] = picked_column(lv_ref[...], first, rows)
         own_energy[...] = picked_column(ve_ref[...], first, rows)
@@ -341,11 +345,9 @@
     left = x - top.astype(F32)
     mid = left.astype(BF16)
     low = (left - mid.astype(F32)).astype(BF16)
-    count = RING * rows
-    three = jnp.dot(
-        jnp.concatenate([top, mid, low], axis=0), hot[...], preferred_element_type=F32
-    )
-    cycle = (three[:count] + three[count : 2 * count]) + three[2 * count :]
+    cycle = jnp.dot(
+        jnp.concatenate([top, mid, low], axis=1), hot[...], preferred_element_type=F32
+    )
     label_i = occ_ref[si_ref[i]]
     energy_i = oe_ref[si_ref[i]]
     label_b = lv_ref[:, cols]
@@ -400,6 +402,12 @@
         for x in range(RING)
         for y in range(RING)
         for c in range(CORES)
+    ]
+
+
+def groups_y():
+    return [
+        [8 * x + 2 * y + c for y in range(RING)] for x in range(RING) for c in range(CORES)
     ]
 
 
@@ -430,41 +438,48 @@
     kept = integrals.shape[3]
     half = 128
     n_rest = n_i + n_i // 2
-    n_cols = RING * CORES * PART
+    n_cols = RING * CORES * PART // CHUNKS
     lv = virt_irrep.reshape(1, wide)
     ve = virt_energy.reshape(1, wide)
     row_spec = whole((1, wide))
-    params = pltpu.CompilerParams(vmem_limit_bytes=48 * 1024 * 1024)
-
-    pa, *pb = pl.pallas_call(
-        pack_kernel,
+    params = pltpu.CompilerParams(vmem_limit_bytes=32 * 1024 * 1024)
+
+    block = pl.BlockSpec((1, n_i, rows, wide), lambda k: (k, 0, 0, 0))
+    pb = pl.pallas_call(
+        pack_dressed_kernel,
         grid=(n_k,),
-        out_shape=[jax.ShapeDtypeStruct((n_k, n_rest, rows, half), BF16)]
-        + [jax.ShapeDtypeStruct((n_k, rows, n_cols), BF16)] * RING,
-        in_specs=[SMEM] * 4
-        + [row_spec] * 3
-        + [pl.BlockSpec((1, n_i, rows, wide), lambda k: (k, 0, 0, 0))] * 2,
-        out_specs=[pl.BlockSpec((1, n_rest, rows, half), lambda k: (k, 0, 0, 0))]
-        + [pl.BlockSpec((1, rows, n_cols), lambda k: (k, 0, 0))] * RING,
+        out_shape=[jax.ShapeDtypeStruct((CHUNKS, n_k, rows, n_cols), BF16)] * RING,
+        in_specs=[SMEM] * 3 + [row_spec] * 2 + [block],
+        out_specs=[pl.BlockSpec((CHUNKS, 1, rows, n_cols), lambda k: (0, k, 0, 0))] * RING,
         scratch_shapes=[
-            pltpu.VMEM((half, wide), BF16),
-            pltpu.VMEM((half, wide), BF16),
-            pltpu.VMEM((half, wide), BF16),
             pltpu.VMEM((RING * PART, wide), BF16),
             pltpu.VMEM((rows, 1), I32),
             pltpu.VMEM((n_i * rows, wide), BF16),
         ],
         compiler_params=params,
-        cost_estimate=cost(2 * 2 * n_k * n_i * rows * wide * 256, 5 << 20),
-        name="pack",
-    )(occ_irrep, slab_i, slab_j, slab_k, lv, rank, part, amplitudes, dressed)
-
-    pb_y = [pb[0]] + [lax.ppermute(pb[d], "blk", ring_y(d)) for d in (1, 3, 2)]
-    pb_y = [pb_y[0], pb_y[1], pb_y[3], pb_y[2]]
-    mine = jnp.stack(pb_y)
-    pa_y = [pa] + [lax.ppermute(pa, "blk", ring_y(d)) for d in (1, 2, 3)]
-    across = [mine] + [lax.ppermute(mine, "blk", ring_x(d)) for d in (1, 2, 3)]
-    twin = [lax.ppermute(b, "blk", other_core()) for b in across]
+        cost_estimate=cost(2 * n_k * n_i * rows * wide * 256, 10 << 20),
+        name="pack_dressed",
+    )(occ_irrep, slab_j, slab_k, lv, part, dressed)
+    pa = pl.pallas_call(
+        pack_amplitudes_kernel,
+        grid=(n_k,),
+        out_shape=jax.ShapeDtypeStruct((RING, n_k, n_rest, rows, half), BF16),
+        in_specs=[SMEM] * 3 + [row_spec] * 2 + [block],
+        out_specs=pl.BlockSpec((RING, 1, n_rest, rows, half), lambda k: (0, k, 0, 0, 0)),
+        scratch_shapes=[
+            pltpu.VMEM((half, wide), BF16),
+            pltpu.VMEM((half, wide), BF16),
+            pltpu.VMEM((half, wide), BF16),
+            pltpu.VMEM((rows, 1), I32),
+            pltpu.VMEM((n_i * rows, wide), BF16),
+        ],
+        compiler_params=params,
+        cost_estimate=cost(2 * n_k * n_i * rows * wide * 256, 10 << 20),
+        name="pack_amplitudes",
+    )(occ_irrep, slab_i, slab_k, lv, rank, amplitudes)
+
+    pb_y = [pb[0]] + [lax.ppermute(pb[d], "blk", ring_y(d)) for d in (1, 2, 3)]
+    pa_y = lax.all_to_all(pa, "blk", 0, 0, axis_index_groups=groups_y())
 
     m_rows = RING * n_i * rows
     spread = pl.pallas_call(
@@ -473,41 +488,53 @@
         out_shape=jax.ShapeDtypeStruct((n_k, m_rows, wide), BF16),
         in_specs=[SMEM] * 3
         + [row_spec] * 2
-        + [pl.BlockSpec((1, n_rest, rows, half), lambda k: (k, 0, 0, 0))] * RING,
+        + [pl.BlockSpec((RING, 1, n_rest, rows, half), lambda k: (0, k, 0, 0, 0))],
         out_specs=pl.BlockSpec((1, m_rows, wide), lambda k: (k, 0, 0)),
         scratch_shapes=[
             pltpu.VMEM((2 * half, wide), BF16),
             pltpu.VMEM((2 * half, wide), BF16),
-            pltpu.VMEM((1, wide), I32),
+            pltpu.VMEM((1, wide), BF16),
             pltpu.VMEM((RING, rows, 1), I32),
         ],
         compiler_params=params,
-        cost_estimate=cost(2 * n_k * m_rows * wide * 256, 10 << 20),
+        cost_estimate=cost(2 * n_k * m_rows * wide * 256, 20 << 20),
         name="unpack",
-    )(occ_irrep, slab_i, slab_k, lv, rank, *pa_y)
-
-    parts = pl.pallas_call(
-        cycle_kernel,
-        grid=(n_k,),
-        out_shape=[jax.ShapeDtypeStruct((m_rows, CORES * PART), F32)] * RING,
-        in_specs=[pl.BlockSpec((1, m_rows, wide), lambda k: (k, 0, 0))]
-        + [pl.BlockSpec((RING, 1, rows, n_cols), lambda k: (0, k, 0, 0))] * 8,
-        out_specs=[pl.BlockSpec((m_rows, CORES * PART), lambda k: (0, 0))] * RING,
-        scratch_shapes=[pltpu.VMEM((wide, n_cols), BF16), pltpu.VMEM((m_rows, n_cols), F32)],
-        compiler_params=params,
-        cost_estimate=cost(2 * n_k * m_rows * wide * n_cols, 14 << 20),
-        name="cycle",
-    )(spread, *across, *twin)
+    )(occ_irrep, slab_i, slab_k, lv, rank, pa_y)
+
+    parts = {}
+    for chunk, steps in enumerate(STEPS):
+        mine = jnp.stack([b[chunk] for b in pb_y])
+        if chunk == 0:
+            mine, pa = lax.optimization_barrier((mine, pa))
+        across = [mine] + [lax.ppermute(mine, "blk", ring_x(d)) for d in (1, 2, 3)]
+        if chunk:
+            across[1:] = lax.optimization_barrier((across[1:], parts[STEPS[0][0]]))[0]
+        twin = [lax.ppermute(b, "blk", other_core()) for b in across]
+        parts[steps[0]], parts[steps[1]] = pl.pallas_call(
+            cycle_kernel,
+            grid=(n_k,),
+            out_shape=[jax.ShapeDtypeStruct((m_rows, CORES * PART), F32)] * 2,
+            in_specs=[pl.BlockSpec((1, m_rows, wide), lambda k: (k, 0, 0))]
+            + [pl.BlockSpec((RING, 1, rows, n_cols), lambda k: (0, k, 0, 0))] * 8,
+            out_specs=[pl.BlockSpec((m_rows, CORES * PART), lambda k: (0, 0))] * 2,
+            scratch_shapes=[pltpu.VMEM((wide, n_cols), BF16), pltpu.VMEM((m_rows, n_cols), F32)],
+            compiler_params=params,
+            cost_estimate=cost(2 * n_k * m_rows * wide * n_cols, 14 << 20),
+            name="cycle",
+        )(spread, *across, *twin)
 
     sums = [parts[0]] + [lax.ppermute(parts[d], "red", ring_z(d)) for d in (1, 2, 3)]
+    lanes = CORES * PART
     terms = pl.pallas_call(
         sum_kernel,
-        out_shape=[jax.ShapeDtypeStruct((n_i, rows, CORES * PART), F32)] * RING,
-        in_specs=[pl.BlockSpec(memory_space=pltpu.VMEM)] * RING,
-        out_specs=[pl.BlockSpec(memory_space=pltpu.VMEM)] * RING,
+        grid=(2,),
+        out_shape=[jax.ShapeDtypeStruct((n_i, rows, lanes), F32)] * RING,
+        in_specs=[pl.BlockSpec((RING, n_i // 2, rows, lanes), lambda n: (0, n, 0, 0))] * RING,
+        out_specs=[pl.BlockSpec((n_i // 2, rows, lanes), lambda n: (n, 0, 0))] * RING,
+        compiler_params=params,
         cost_estimate=cost(m_rows * 512, 3 << 20),
         name="sums",
-    )(*sums)
+    )(*[o.reshape(RING, n_i, rows, lanes) for o in sums])
     back = [terms[0]] + [lax.ppermute(terms[d], "blk", ring_y(RING - d)) for d in (1, 2, 3)]
 
     return pl.pallas_call(
@@ -520,7 +547,7 @@
         + [pl.BlockSpec((1, n_j, rows, kept), lambda i: (i, 0, 0, 0))],
         out_specs=pl.BlockSpec((1, n_j, rows, kept), lambda i: (i, 0, 0, 0)),
         scratch_shapes=[
-            pltpu.VMEM((CORES * PART, CORES * kept), BF16),
+            pltpu.VMEM((3 * CORES * PART, CORES * kept), BF16),
             pltpu.VMEM((rows, 1), I32),
             pltpu.VMEM((rows, 1), F32),
         ],

time: 125 us -> 99.1 us (0.79)
  waiting for transfers between devices: 49.1 us -> 35.4 us
  between operations: 14 us -> 0.66 us
  starting transfers between devices: 28.2 us -> 33.2 us
  local copies, waits for them, and re-layouts: 4.84 us -> 1.52 us
  Pallas kernels: 28.2 us -> 26.8 us
    ppermute x6 -> x3, waiting for transfers between devices: 18.6 us -> 0.01 us  [packed_form(): pb_y = [pb[0]] + [lax.ppermute(pb[d], 'blk', ring_y(d)) for d in (1, 2, 3)]]
    ppermute x3 -> x6, waiting for transfers between devices: 0.62 us -> 10.2 us  [packed_form(): across = [mine] + [lax.ppermute(mine, 'blk', ring_x(d)) for d in (1, 2, 3)]]
    ppermute x6 -> x3, starting transfers between devices: 11.5 us -> 5.98 us  [packed_form(): pb_y = [pb[0]] + [lax.ppermute(pb[d], 'blk', ring_y(d)) for d in (1, 2, 3)]]
    ppermute x3 -> x6, starting transfers between devices: 5.72 us -> 10.7 us  [packed_form(): across = [mine] + [lax.ppermute(mine, 'blk', ring_x(d)) for d in (1, 2, 3)]]
    ppermute x3, waiting for transfers between devices: 22.1 us -> 17.7 us  [packed_form(): lax.ppermute(parts[d], 'red', ring_z(d))]
    all_to_all x0 -> x1, starting transfers between devices: none -> 3.56 us  [packed_form(): pa_y = lax.all_to_all(pa, 'blk', 0, 0, axis_index_groups=groups_y())]
    cond x28 -> x26, local copies, waits for them, and re-layouts: 3.53 us -> 1.48 us
    pallas_call x1, Pallas kernels: 3.14 us -> 4.96 us  [packed_form(): pl.pallas_call(update_kernel, grid=(n_i,), out_shape=jax.ShapeDtypeStruct...]
  transfers between devices with their start and end apart: 19 -> 24, of which waited for: 10 -> 9; matrix products, arithmetic and copies ran while one was open for 0% -> 0% of each run, Pallas kernels for 5% -> 17%
where the time goes in v2:
time: 99.1 us; the launch traced here: 98.2 us
  waiting for transfers between devices  35.4 us (36%)
  starting transfers between devices  33.2 us (34%)
  Pallas kernels  26.8 us (27%)
  local copies, waits for them, and re-layouts  1.52 us (2%)
    ppermute x3, waiting for transfers between devices, packed_form(): lax.ppermute(parts[d], 'red', ring_z(d))  17.7 us
    ppermute x6, starting transfers between devices, packed_form(): across = [mine] + [lax.ppermute(mine, 'blk', ring_x(d)) for d in (1, 2, 3)]  10.7 us
    ppermute x6, waiting for transfers between devices, packed_form(): across = [mine] + [lax.ppermute(mine, 'blk', ring_x(d)) for d in (1, 2, 3)]  10.2 us
    pallas_call x2, Pallas kernels, packed_form(): pl.pallas_call(cycle_kernel, grid=(n_k,), out_shape=[jax.ShapeDtypeStruct...  7.89 us
    ppermute x3, waiting for transfers between devices, packed_form(): lax.ppermute(terms[d], 'blk', ring_y(RING - d))  7.45 us
    ppermute x3, starting transfers between devices, packed_form(): lax.ppermute(parts[d], 'red', ring_z(d))  7.18 us
    ppermute x3, starting transfers between devices, packed_form(): pb_y = [pb[0]] + [lax.ppermute(pb[d], 'blk', ring_y(d)) for d in (1, 2, 3)]  5.98 us
    pallas_call x1, Pallas kernels, packed_form(): pl.pallas_call(update_kernel, grid=(n_i,), out_shape=jax.ShapeDtypeStruct...  4.96 us
  transfers between devices with their start and end apart: 24, of which 9 were waited for; matrix products, arithmetic and copies ran while one was open for 0% of the time, Pallas kernels for 17%

profile of v2, /device:TPU:0, one launch (start us, length us, event | category | flops | bytes accessed | tf_op | source)
XLA Modules:
  0.0 98.2 jit_solution(14881975087186352192)
XLA Ops:
  0.0 1.4 %ranks.1 = (s32[1,1024]{1,0:T(1,128)S(1)}, s32[1,1024]{1,0:T(1,128)S(1)}, s32[1]{0:T(128)}) custom-call(s32[1,1024]{1,0:T(1,128)} %bitcast.55), custom_call_target="tpu_custom_call" | custom-call | tf_op jit(solution)/shard_map/ranks/pallas_call | solution.py:380
  2.0 96.2 %conditional.1 = (f32[8,8,32,256]{3,2,1,0:T(8,128)}) conditional(s32[]{:T(128)} %bitcast.25, (s32[8]{0:T(128)}, s32[200]{0:T(256)}, s32[8]{0:T(128)}, s32[1024]{0:T(1024)}, bf16[8,8,32,256]{3,2,1,0:T(8,128)(2,1)}, /*index=5*/(), s32[4]{0:T(128)}, bf16[4,8,32,1024]{3,2,1,0:T(8,128)(2,1)}, (), bf16[4,8,32,1024]{3,2,1,0:T(8,128)(2,1)}, ...), branch_computations={%region_0.7_spmd, %region_7.8_spmd} | conditional | flops 17191471104 | bytes 324383456 | solution.py:563
  2.3 0.0 copy-start.4
  2.3 0.0 copy-start.7
  2.3 0.0 copy-start.8
  2.3 0.0 copy-start.10
  2.3 0.0 copy-start.11
  2.3 3.9 %pack_dressed.1 = (bf16[2,4,32,256]{3,2,1,0:T(8,128)(2,1)S(1)}, bf16[2,4,32,256]{3,2,1,0:T(8,128)(2,1)S(1)}, bf16[2,4,32,256]{3,2,1,0:T(8,128)(2,1)S(1)}, bf16[2,4,32,256]{3,2,1,0:T(8,128)(2,1)S(1)}) custom-call(s32[200]{0:T(256)} %get-tuple-element.68.occ_ref, s32[8]{0:T(128)} %get-tuple-element.70.sj_ref, s32[4]{0:T(128)} %get-tuple-element.75.sk_ref, ...), custom_call_target="tpu_custom_call" | custom-call | flops 536870912 | bytes 10485760 | tf_op jit(solution)/shard_map/cond/branch_1_fun/pack_dressed/pallas_call | solution.py:448
  6.3 1.7 %collective-permute-start = (bf16[2,4,32,256]{3,2,1,0:T(8,128)(2,1)S(1)}, bf16[2,4,32,256]{3,2,1,0:T(8,128)(2,1)S(1)}, u32[]{:S(2)}, u32[]{:S(2)}) collective-permute-start(bf16[2,4,32,256]{3,2,1,0:T(8,128)(2,1)S(1)} %get-tuple-element.80), channel_id=1, source_target_pairs={{0,8},{4,12},{8,16},{12,20},{16,24},{20,28},{24,0},{28,4},{32,40},... | collective-permute-start | bytes 393224 | tf_op jit(solution)/shard_map/cond/branch_1_fun/ppermute | solution.py:481
  8.0 2.9 %collective-permute-start.1 = (bf16[2,4,32,256]{3,2,1,0:T(8,128)(2,1)S(1)}, bf16[2,4,32,256]{3,2,1,0:T(8,128)(2,1)S(1)}, u32[]{:S(2)}, u32[]{:S(2)}) collective-permute-start(bf16[2,4,32,256]{3,2,1,0:T(8,128)(2,1)S(1)} %get-tuple-element.81), channel_id=1, source_target_pairs={{0,16},{4,20},{8,24},{12,28},{16,0},{20,4},{24,8},{28,12},{32,48},... | collective-permute-start | bytes 393224 | tf_op jit(solution)/shard_map/cond/branch_1_fun/ppermute | solution.py:481
  10.9 1.3 %collective-permute-start.2 = (bf16[2,4,32,256]{3,2,1,0:T(8,128)(2,1)S(1)}, bf16[2,4,32,256]{3,2,1,0:T(8,128)(2,1)S(1)}, u32[]{:S(2)}, u32[]{:S(2)}) collective-permute-start(bf16[2,4,32,256]{3,2,1,0:T(8,128)(2,1)S(1)} %get-tuple-element.82), channel_id=1, source_target_pairs={{0,24},{4,28},{8,0},{12,4},{16,8},{20,12},{24,16},{28,20},{32,56},... | collective-permute-start | bytes 393224 | tf_op jit(solution)/shard_map/cond/branch_1_fun/ppermute | solution.py:481
  12.3 3.7 %pack_amplitudes.1 = bf16[4,4,12,32,128]{4,3,2,1,0:T(8,128)(2,1)} custom-call(s32[200]{0:T(256)S(1)} %copy-done.8, s32[8]{0:T(128)S(1)} %copy-done.10, s32[4]{0:T(128)S(1)} %copy-done.11, s32[1,1024]{1,0:T(1,128)S(1)} %bitcast.57, s32[1,1024]{1,0:T(1,128)S(1)} %get-tuple-element.76.rank_ref, bf16[4,8,32,1024]{3,2,1,0:T(8,128)(2,1)S(1)} %copy-done.4), custom_call_target="tpu_custom_call" | custom-call | flops 536870912 | bytes 10485760 | tf_op jit(solution)/shard_map/cond/branch_1_fun/pack_amplitudes/pallas_call | solution.py:463
  16.0 3.6 %all-to-all-start = ((bf16[4,4,12,32,128]{4,3,2,1,0:T(8,128)(2,1)}), bf16[4,4,12,32,128]{4,3,2,1,0:T(8,128)(2,1)S(1)}, u32[]{:S(2)}, u32[]{:S(2)}) async-start(bf16[4,4,12,32,128]{4,3,2,1,0:T(8,128)(2,1)} %pack_amplitudes.1), calls=%async_computation | async-start | bytes 3145728 | tf_op jit(solution)/shard_map/cond/branch_1_fun/all_to_all | solution.py:482
  19.6 0.0 collective-permute-done
  19.7 1.6 %collective-permute-start.6 = (bf16[4,4,32,256]{3,2,1,0:T(8,128)(2,1)S(1)}, bf16[4,4,32,256]{3,2,1,0:T(8,128)(2,1)S(1)}, u32[]{:S(2)}, u32[]{:S(2)}) collective-permute-start(bf16[4,4,32,256]{3,2,1,0:T(8,128)(2,1)S(1)} %pad_maximum_fusion.1.b0), channel_id=1, source_target_pairs={{0,32},{4,36},{8,40},{12,44},{16,48},{20,52},{24,56},{28,60},{32,6... | collective-permute-start | bytes 786440 | tf_op jit(solution)/shard_map/cond/branch_1_fun/ppermute | solution.py:509
  21.3 2.7 %collective-permute-start.7 = (bf16[4,4,32,256]{3,2,1,0:T(8,128)(2,1)S(1)}, bf16[4,4,32,256]{3,2,1,0:T(8,128)(2,1)S(1)}, u32[]{:S(2)}, u32[]{:S(2)}) collective-permute-start(bf16[4,4,32,256]{3,2,1,0:T(8,128)(2,1)S(1)} %pad_maximum_fusion.1.b0), channel_id=1, source_target_pairs={{0,64},{4,68},{8,72},{12,76},{16,80},{20,84},{24,88},{28,92},{32,9... | collective-permute-start | bytes 786440 | tf_op jit(solution)/shard_map/cond/branch_1_fun/ppermute | solution.py:509
  24.0 1.4 %collective-permute-start.8 = (bf16[4,4,32,256]{3,2,1,0:T(8,128)(2,1)S(1)}, bf16[4,4,32,256]{3,2,1,0:T(8,128)(2,1)}, u32[]{:S(2)}, u32[]{:S(2)}) collective-permute-start(bf16[4,4,32,256]{3,2,1,0:T(8,128)(2,1)S(1)} %pad_maximum_fusion.1.b0), channel_id=1, source_target_pairs={{0,96},{4,100},{8,104},{12,108},{16,112},{20,116},{24,120},{28,124... | collective-permute-start | bytes 786440 | tf_op jit(solution)/shard_map/cond/branch_1_fun/ppermute | solution.py:509
  25.4 0.0 collective-permute-start.9
  25.4 3.8 %collective-permute-done.6.b1 = bf16[4,4,32,256]{3,2,1,0:T(8,128)(2,1)S(1)} collective-permute-done((bf16[4,4,32,256]{3,2,1,0:T(8,128)(2,1)S(1)}, bf16[4,4,32,256]{3,2,1,0:T(8,128)(2,1)S(1)}, u32[]{:S(2)}, u32[]{:S(2)}) %collective-permute-start.6) | collective-permute-done | bytes 262176 | tf_op jit(solution)/shard_map/cond/branch_1_fun/ppermute | solution.py:509
  29.2 0.0 collective-permute-start.10
  29.2 5.6 %collective-permute-done.7.b2 = bf16[4,4,32,256]{3,2,1,0:T(8,128)(2,1)S(1)} collective-permute-done((bf16[4,4,32,256]{3,2,1,0:T(8,128)(2,1)S(1)}, bf16[4,4,32,256]{3,2,1,0:T(8,128)(2,1)S(1)}, u32[]{:S(2)}, u32[]{:S(2)}) %collective-permute-start.7) | collective-permute-done | bytes 262176 | tf_op jit(solution)/shard_map/cond/branch_1_fun/ppermute | solution.py:509
  34.8 0.0 collective-permute-start.11
  34.8 0.0 collective-permute-done.8.b3
  34.8 0.5 collective-permute-start.12
  35.3 1.0 %collective-permute-start.3 = (bf16[4,4,32,256]{3,2,1,0:T(8,128)(2,1)S(1)}, bf16[4,4,32,256]{3,2,1,0:T(8,128)(2,1)S(1)}, u32[]{:S(2)}, u32[]{:S(2)}) collective-permute-start(bf16[4,4,32,256]{3,2,1,0:T(8,128)(2,1)S(1)} %pad_maximum_fusion.b0), channel_id=1, source_target_pairs={{0,32},{4,36},{8,40},{12,44},{16,48},{20,52},{24,56},{28,60},{32,6... | collective-permute-start | bytes 786440 | tf_op jit(solution)/shard_map/cond/branch_1_fun/ppermute | solution.py:509
  36.3 0.0 collective-permute-done.9.b4
  36.3 0.7 copy-done
  37.0 2.4 %collective-permute-start.4 = (bf16[4,4,32,256]{3,2,1,0:T(8,128)(2,1)S(1)}, bf16[4,4,32,256]{3,2,1,0:T(8,128)(2,1)S(1)}, u32[]{:S(2)}, u32[]{:S(2)}) collective-permute-start(bf16[4,4,32,256]{3,2,1,0:T(8,128)(2,1)S(1)} %pad_maximum_fusion.b0), channel_id=1, source_target_pairs={{0,64},{4,68},{8,72},{12,76},{16,80},{20,84},{24,88},{28,92},{32,9... | collective-permute-start | bytes 786440 | tf_op jit(solution)/shard_map/cond/branch_1_fun/ppermute | solution.py:509
  39.4 0.0 collective-permute-done.10.b5
  39.4 0.7 copy-done.2
  40.2 1.6 %collective-permute-start.5 = (bf16[4,4,32,256]{3,2,1,0:T(8,128)(2,1)S(1)}, bf16[4,4,32,256]{3,2,1,0:T(8,128)(2,1)S(1)}, u32[]{:S(2)}, u32[]{:S(2)}) collective-permute-start(bf16[4,4,32,256]{3,2,1,0:T(8,128)(2,1)S(1)} %pad_maximum_fusion.b0), channel_id=1, source_target_pairs={{0,96},{4,100},{8,104},{12,108},{16,112},{20,116},{24,120},{28,124... | collective-permute-start | bytes 786440 | tf_op jit(solution)/shard_map/cond/branch_1_fun/ppermute | solution.py:509
  41.7 0.0 all-to-all-done.pa_ref
  41.7 4.6 %unpack.1.a_ref = bf16[4,1024,1024]{2,1,0:T(8,128)(2,1)S(1)} custom-call(s32[200]{0:T(256)S(1)} %copy-done.8, s32[8]{0:T(128)S(1)} %copy-done.10, s32[4]{0:T(128)S(1)} %copy-done.11, s32[1,1024]{1,0:T(1,128)S(1)} %bitcast.58, s32[1,1024]{1,0:T(1,128)S(1)} %get-tuple-element.76.rank_ref, bf16[4,4,12,32,128]{4,3,2,1,0:T(8,128)(2,1)S(1)} %all-to-all-done.pa_ref), custom_call_target="tpu_custom_call" | custom-call | flops 2147483648 | bytes 20971520 | tf_op jit(solution)/shard_map/cond/branch_1_fun/unpack/pallas_call | solution.py:485
  46.4 0.0 collective-permute-done.11.b6
  46.4 0.1 collective-permute-start.13
  46.5 0.0 collective-permute-done.12.b7
  46.5 4.4 %cycle.2 = (f32[1024,128]{1,0:T(8,128)S(1)}, f32[1024,128]{1,0:T(8,128)S(1)}) custom-call(bf16[4,1024,1024]{2,1,0:T(8,128)(2,1)S(1)} %unpack.1.a_ref, bf16[4,4,32,256]{3,2,1,0:T(8,128)(2,1)S(1)} %pad_maximum_fusion.1.b0, bf16[4,4,32,256]{3,2,1,0:T(8,128)(2,1)S(1)} %collective-permute-done.6.b1, bf16[4,4,32,256]{3,2,1,0:T(8,128)(2,1)S(1)} %collective-permute-done.7.b2, ...), custom_call_target="tpu_custom_call" | custom-call | flops 2147483648 | bytes 14680064 | tf_op jit(solution)/shard_map/cond/branch_1_fun/cycle/pallas_call | solution.py:513
  50.9 0.0 collective-permute-done.3.b1
  50.9 0.1 collective-permute-done.4.b2
  51.0 0.7 collective-permute-done.5.b3
  51.8 0.0 collective-permute-start.14
  51.8 0.5 collective-permute-start.15
  52.3 0.0 collective-permute-start.16
  52.3 3.9 %collective-permute-start.18 = (f32[1024,128]{1,0:T(8,128)S(1)}, f32[1024,128]{1,0:T(8,128)S(1)}, u32[]{:S(2)}, u32[]{:S(2)}) collective-permute-start(f32[1024,128]{1,0:T(8,128)S(1)} %get-tuple-element.84), channel_id=1, source_target_pairs={{0,2},{1,3},{2,0},{3,1},{4,6},{5,7},{6,4},{7,5},{8,10},{9,11},{10,... | collective-permute-start | bytes 1572872 | tf_op jit(solution)/shard_map/cond/branch_1_fun/ppermute | solution.py:526
  56.2 0.0 collective-permute-done.13.b4
  56.2 1.0 %collective-permute-start.17 = (f32[1024,128]{1,0:T(8,128)S(1)}, f32[1024,128]{1,0:T(8,128)S(1)}, u32[]{:S(2)}, u32[]{:S(2)}) collective-permute-start(f32[1024,128]{1,0:T(8,128)S(1)} %get-tuple-element.89), channel_id=1, source_target_pairs={{0,1},{1,2},{2,3},{3,0},{4,5},{5,6},{6,7},{7,4},{8,9},{9,10},{10,1... | collective-permute-start | bytes 1572872 | tf_op jit(solution)/shard_map/cond/branch_1_fun/ppermute | solution.py:526
  57.2 0.0 collective-permute-done.14.b5
  57.2 0.0 collective-permute-done.15.b6
  57.2 3.5 %cycle.3 = (f32[1024,128]{1,0:T(8,128)S(1)}, f32[1024,128]{1,0:T(8,128)S(1)}) custom-call(bf16[4,1024,1024]{2,1,0:T(8,128)(2,1)S(1)} %unpack.1.a_ref, bf16[4,4,32,256]{3,2,1,0:T(8,128)(2,1)S(1)} %pad_maximum_fusion.b0, bf16[4,4,32,256]{3,2,1,0:T(8,128)(2,1)S(1)} %collective-permute-done.3.b1, bf16[4,4,32,256]{3,2,1,0:T(8,128)(2,1)S(1)} %collective-permute-done.4.b2, ...), custom_call_target="tpu_custom_call" | custom-call | flops 2147483648 | bytes 14680064 | tf_op jit(solution)/shard_map/cond/branch_1_fun/cycle/pallas_call | solution.py:513
  60.7 0.0 copy-start.6
  60.7 0.0 copy-start.13
  60.7 0.0 copy-start.14
  60.7 0.0 copy-start.16
  60.7 2.3 %collective-permute-start.19 = (f32[1024,128]{1,0:T(8,128)S(1)}, f32[1024,128]{1,0:T(8,128)S(1)}, u32[]{:S(2)}, u32[]{:S(2)}) collective-permute-start(f32[1024,128]{1,0:T(8,128)S(1)} %get-tuple-element.90), channel_id=1, source_target_pairs={{0,3},{1,0},{2,1},{3,2},{4,7},{5,4},{6,5},{7,6},{8,11},{9,8},{10,9... | collective-permute-start | bytes 1572872 | tf_op jit(solution)/shard_map/cond/branch_1_fun/ppermute | solution.py:526
  63.0 17.0 %collective-permute-done.17 = f32[1024,128]{1,0:T(8,128)S(1)} collective-permute-done((f32[1024,128]{1,0:T(8,128)S(1)}, f32[1024,128]{1,0:T(8,128)S(1)}, u32[]{:S(2)}, u32[]{:S(2)}) %collective-permute-start.17) | collective-permute-done | bytes 524320 | tf_op jit(solution)/shard_map/cond/branch_1_fun/ppermute | solution.py:526
  80.0 0.8 collective-permute-done.19
  80.8 0.3 sums.1
  81.1 3.0 %collective-permute-start.20 = (f32[8,32,128]{2,1,0:T(8,128)S(1)}, f32[8,32,128]{2,1,0:T(8,128)S(1)}, u32[]{:S(2)}, u32[]{:S(2)}) collective-permute-start(f32[8,32,128]{2,1,0:T(8,128)S(1)} %get-tuple-element.92), channel_id=1, source_target_pairs={{0,24},{4,28},{8,0},{12,4},{16,8},{20,12},{24,16},{28,20},{32,56},... | collective-permute-start | bytes 393224 | tf_op jit(solution)/shard_map/cond/branch_1_fun/ppermute | solution.py:538
  84.1 0.9 collective-permute-start.21
  84.9 0.9 collective-permute-start.22
  85.8 3.7 %collective-permute-done.20.t1 = f32[8,32,128]{2,1,0:T(8,128)S(1)} collective-permute-done((f32[8,32,128]{2,1,0:T(8,128)S(1)}, f32[8,32,128]{2,1,0:T(8,128)S(1)}, u32[]{:S(2)}, u32[]{:S(2)}) %collective-permute-start.20) | collective-permute-done | bytes 131104 | tf_op jit(solution)/shard_map/cond/branch_1_fun/ppermute | solution.py:538
  89.5 2.3 %collective-permute-done.21.t2 = f32[8,32,128]{2,1,0:T(8,128)S(1)} collective-permute-done((f32[8,32,128]{2,1,0:T(8,128)S(1)}, f32[8,32,128]{2,1,0:T(8,128)S(1)}, u32[]{:S(2)}, u32[]{:S(2)}) %collective-permute-start.21) | collective-permute-done | bytes 131104 | tf_op jit(solution)/shard_map/cond/branch_1_fun/ppermute | solution.py:538
  91.8 1.4 %collective-permute-done.22.t3 = f32[8,32,128]{2,1,0:T(8,128)S(1)} collective-permute-done((f32[8,32,128]{2,1,0:T(8,128)S(1)}, f32[8,32,128]{2,1,0:T(8,128)S(1)}, u32[]{:S(2)}, u32[]{:S(2)}) %collective-permute-start.22) | collective-permute-done | bytes 131104 | tf_op jit(solution)/shard_map/cond/branch_1_fun/ppermute | solution.py:538
  93.2 5.0 %update.1 = f32[8,8,32,256]{3,2,1,0:T(8,128)} custom-call(s32[200]{0:T(256)S(1)} %copy-done.8, s32[8]{0:T(128)S(1)} %copy-done.10, s32[8]{0:T(128)S(1)} %copy-done.13, f32[200]{0:T(256)S(1)} %copy-done.16, s32[1,1024]{1,0:T(1,128)S(1)} %bitcast.59, f32[1,1024]{1,0:T(1,128)S(1)} %bitcast.60, s32[1,1024]{1,0:T(1,128)S(1)} %get-tuple-element.74.part_ref, ...), custom_call_target="tpu_custom_call" | custom-call | flops 402653184 | bytes 4194304 | tf_op jit(solution)/shard_map/cond/branch_1_fun/update/pallas_call | solution.py:540
  (25 shorter events, 0.2 us)
Async XLA Ops:
  2.3 10.0 %copy-start.4 = (bf16[4,8,32,1024]{3,2,1,0:T(8,128)(2,1)S(1)}, bf16[4,8,32,1024]{3,2,1,0:T(8,128)(2,1)}, u32[]{:S(2)}) copy-start(bf16[4,8,32,1024]{3,2,1,0:T(8,128)(2,1)} %get-tuple-element.77.amp_ref) | copy-start | bytes 6291460 | tf_op jit(solution)/shard_map/cond
  2.3 10.0 %copy-start.7 = (s32[1024]{0:T(1024)S(1)}, s32[1024]{0:T(1024)}, u32[]{:S(2)}) copy-start(s32[1024]{0:T(1024)} %get-tuple-element.72) | copy-start | bytes 12292 | tf_op jit(solution)/shard_map/cond
  2.3 10.0 %copy-start.8 = (s32[200]{0:T(256)S(1)}, s32[200]{0:T(256)}, u32[]{:S(2)}) copy-start(s32[200]{0:T(256)} %get-tuple-element.68.occ_ref) | copy-start | bytes 2404 | tf_op jit(solution)/shard_map/cond
  2.3 10.0 %copy-start.10 = (s32[8]{0:T(128)S(1)}, s32[8]{0:T(128)}, u32[]{:S(2)}) copy-start(s32[8]{0:T(128)} %get-tuple-element.69.si_ref) | copy-start | bytes 100 | tf_op jit(solution)/shard_map/cond
  2.3 9.9 %copy-start.11 = (s32[4]{0:T(128)S(1)}, s32[4]{0:T(128)}, u32[]{:S(2)}) copy-start(s32[4]{0:T(128)} %get-tuple-element.75.sk_ref) | copy-start | bytes 52 | tf_op jit(solution)/shard_map/cond
  6.3 13.3 %collective-permute-start = (bf16[2,4,32,256]{3,2,1,0:T(8,128)(2,1)S(1)}, bf16[2,4,32,256]{3,2,1,0:T(8,128)(2,1)S(1)}, u32[]{:S(2)}, u32[]{:S(2)}) collective-permute-start(bf16[2,4,32,256]{3,2,1,0:T(8,128)(2,1)S(1)} %get-tuple-element.80), channel_id=1, source_target_pairs={{0,8},{4,12},{8,16},{12,20},{16,24},{20,28},{24,0},{28,4},{32,40},... | collective-permute-start | bytes 393224 | tf_op jit(solution)/shard_map/cond/branch_1_fun/ppermute | solution.py:481
  8.0 11.6 %collective-permute-start.1 = (bf16[2,4,32,256]{3,2,1,0:T(8,128)(2,1)S(1)}, bf16[2,4,32,256]{3,2,1,0:T(8,128)(2,1)S(1)}, u32[]{:S(2)}, u32[]{:S(2)}) collective-permute-start(bf16[2,4,32,256]{3,2,1,0:T(8,128)(2,1)S(1)} %get-tuple-element.81), channel_id=1, source_target_pairs={{0,16},{4,20},{8,24},{12,28},{16,0},{20,4},{24,8},{28,12},{32,48},... | collective-permute-start | bytes 393224 | tf_op jit(solution)/shard_map/cond/branch_1_fun/ppermute | solution.py:481
  10.9 8.7 %collective-permute-start.2 = (bf16[2,4,32,256]{3,2,1,0:T(8,128)(2,1)S(1)}, bf16[2,4,32,256]{3,2,1,0:T(8,128)(2,1)S(1)}, u32[]{:S(2)}, u32[]{:S(2)}) collective-permute-start(bf16[2,4,32,256]{3,2,1,0:T(8,128)(2,1)S(1)} %get-tuple-element.82), channel_id=1, source_target_pairs={{0,24},{4,28},{8,0},{12,4},{16,8},{20,12},{24,16},{28,20},{32,56},... | collective-permute-start | bytes 393224 | tf_op jit(solution)/shard_map/cond/branch_1_fun/ppermute | solution.py:481
  16.0 25.8 %all-to-all-start = ((bf16[4,4,12,32,128]{4,3,2,1,0:T(8,128)(2,1)}), bf16[4,4,12,32,128]{4,3,2,1,0:T(8,128)(2,1)S(1)}, u32[]{:S(2)}, u32[]{:S(2)}) async-start(bf16[4,4,12,32,128]{4,3,2,1,0:T(8,128)(2,1)} %pack_amplitudes.1), calls=%async_computation | async-start | bytes 3145728 | tf_op jit(solution)/shard_map/cond/branch_1_fun/all_to_all | solution.py:482
  19.7 9.5 %collective-permute-start.6 = (bf16[4,4,32,256]{3,2,1,0:T(8,128)(2,1)S(1)}, bf16[4,4,32,256]{3,2,1,0:T(8,128)(2,1)S(1)}, u32[]{:S(2)}, u32[]{:S(2)}) collective-permute-start(bf16[4,4,32,256]{3,2,1,0:T(8,128)(2,1)S(1)} %pad_maximum_fusion.1.b0), channel_id=1, source_target_pairs={{0,32},{4,36},{8,40},{12,44},{16,48},{20,52},{24,56},{28,60},{32,6... | collective-permute-start | bytes 786440 | tf_op jit(solution)/shard_map/cond/branch_1_fun/ppermute | solution.py:509
  21.3 13.5 %collective-permute-start.7 = (bf16[4,4,32,256]{3,2,1,0:T(8,128)(2,1)S(1)}, bf16[4,4,32,256]{3,2,1,0:T(8,128)(2,1)S(1)}, u32[]{:S(2)}, u32[]{:S(2)}) collective-permute-start(bf16[4,4,32,256]{3,2,1,0:T(8,128)(2,1)S(1)} %pad_maximum_fusion.1.b0), channel_id=1, source_target_pairs={{0,64},{4,68},{8,72},{12,76},{16,80},{20,84},{24,88},{28,92},{32,9... | collective-permute-start | bytes 786440 | tf_op jit(solution)/shard_map/cond/branch_1_fun/ppermute | solution.py:509
  24.0 10.8 %collective-permute-start.8 = (bf16[4,4,32,256]{3,2,1,0:T(8,128)(2,1)S(1)}, bf16[4,4,32,256]{3,2,1,0:T(8,128)(2,1)}, u32[]{:S(2)}, u32[]{:S(2)}) collective-permute-start(bf16[4,4,32,256]{3,2,1,0:T(8,128)(2,1)S(1)} %pad_maximum_fusion.1.b0), channel_id=1, source_target_pairs={{0,96},{4,100},{8,104},{12,108},{16,112},{20,116},{24,120},{28,124... | collective-permute-start | bytes 786440 | tf_op jit(solution)/shard_map/cond/branch_1_fun/ppermute | solution.py:509
  25.4 10.9 %collective-permute-start.9 = (bf16[4,4,32,256]{3,2,1,0:T(8,128)(2,1)S(1)}, bf16[4,4,32,256]{3,2,1,0:T(8,128)(2,1)S(1)}, u32[]{:S(2)}, u32[]{:S(2)}) collective-permute-start(bf16[4,4,32,256]{3,2,1,0:T(8,128)(2,1)S(1)} %pad_maximum_fusion.1.b0), channel_id=1, source_target_pairs={{0,4},{4,0},{8,12},{12,8},{16,20},{20,16},{24,28},{28,24},{32,36},... | collective-permute-start | bytes 786440 | tf_op jit(solution)/shard_map/cond/branch_1_fun/ppermute | solution.py:512
  29.2 10.2 %collective-permute-start.10 = (bf16[4,4,32,256]{3,2,1,0:T(8,128)(2,1)S(1)}, bf16[4,4,32,256]{3,2,1,0:T(8,128)(2,1)S(1)}, u32[]{:S(2)}, u32[]{:S(2)}) collective-permute-start(bf16[4,4,32,256]{3,2,1,0:T(8,128)(2,1)S(1)} %collective-permute-done.6.b1), channel_id=1, source_target_pairs={{0,4},{4,0},{8,12},{12,8},{16,20},{20,16},{24,28},{28,24},{32,36},... | collective-permute-start | bytes 786440 | tf_op jit(solution)/shard_map/cond/branch_1_fun/ppermute | solution.py:512
  34.8 11.6 %collective-permute-start.11 = (bf16[4,4,32,256]{3,2,1,0:T(8,128)(2,1)S(1)}, bf16[4,4,32,256]{3,2,1,0:T(8,128)(2,1)}, u32[]{:S(2)}, u32[]{:S(2)}) collective-permute-start(bf16[4,4,32,256]{3,2,1,0:T(8,128)(2,1)S(1)} %collective-permute-done.7.b2), channel_id=1, source_target_pairs={{0,4},{4,0},{8,12},{12,8},{16,20},{20,16},{24,28},{28,24},{32,36},... | collective-permute-start | bytes 786440 | tf_op jit(solution)/shard_map/cond/branch_1_fun/ppermute | solution.py:512
  34.8 11.7 %collective-permute-start.12 = (bf16[4,4,32,256]{3,2,1,0:T(8,128)(2,1)}, bf16[4,4,32,256]{3,2,1,0:T(8,128)(2,1)}, u32[]{:S(2)}, u32[]{:S(2)}) collective-permute-start(bf16[4,4,32,256]{3,2,1,0:T(8,128)(2,1)} %collective-permute-done.8.b3), channel_id=1, source_target_pairs={{0,4},{4,0},{8,12},{12,8},{16,20},{20,16},{24,28},{28,24},{32,36},... | collective-permute-start | bytes 786440 | tf_op jit(solution)/shard_map/cond/branch_1_fun/ppermute | solution.py:512
  35.3 15.6 %collective-permute-start.3 = (bf16[4,4,32,256]{3,2,1,0:T(8,128)(2,1)S(1)}, bf16[4,4,32,256]{3,2,1,0:T(8,128)(2,1)S(1)}, u32[]{:S(2)}, u32[]{:S(2)}) collective-permute-start(bf16[4,4,32,256]{3,2,1,0:T(8,128)(2,1)S(1)} %pad_maximum_fusion.b0), channel_id=1, source_target_pairs={{0,32},{4,36},{8,40},{12,44},{16,48},{20,52},{24,56},{28,60},{32,6... | collective-permute-start | bytes 786440 | tf_op jit(solution)/shard_map/cond/branch_1_fun/ppermute | solution.py:509
  36.3 0.7 copy-start
  37.0 14.0 %collective-permute-start.4 = (bf16[4,4,32,256]{3,2,1,0:T(8,128)(2,1)S(1)}, bf16[4,4,32,256]{3,2,1,0:T(8,128)(2,1)S(1)}, u32[]{:S(2)}, u32[]{:S(2)}) collective-permute-start(bf16[4,4,32,256]{3,2,1,0:T(8,128)(2,1)S(1)} %pad_maximum_fusion.b0), channel_id=1, source_target_pairs={{0,64},{4,68},{8,72},{12,76},{16,80},{20,84},{24,88},{28,92},{32,9... | collective-permute-start | bytes 786440 | tf_op jit(solution)/shard_map/cond/branch_1_fun/ppermute | solution.py:509
  39.4 0.7 copy-start.2
  40.2 11.6 %collective-permute-start.5 = (bf16[4,4,32,256]{3,2,1,0:T(8,128)(2,1)S(1)}, bf16[4,4,32,256]{3,2,1,0:T(8,128)(2,1)S(1)}, u32[]{:S(2)}, u32[]{:S(2)}) collective-permute-start(bf16[4,4,32,256]{3,2,1,0:T(8,128)(2,1)S(1)} %pad_maximum_fusion.b0), channel_id=1, source_target_pairs={{0,96},{4,100},{8,104},{12,108},{16,112},{20,116},{24,120},{28,124... | collective-permute-start | bytes 786440 | tf_op jit(solution)/shard_map/cond/branch_1_fun/ppermute | solution.py:509
  41.7 4.7 %copy-start.1 = (bf16[4,4,32,256]{3,2,1,0:T(8,128)(2,1)S(1)}, bf16[4,4,32,256]{3,2,1,0:T(8,128)(2,1)}, u32[]{:S(2)}) copy-start(bf16[4,4,32,256]{3,2,1,0:T(8,128)(2,1)} %copy-done) | copy-start | bytes 786436 | tf_op jit(solution)/shard_map/cond
  41.7 4.8 %copy-start.3 = (bf16[4,4,32,256]{3,2,1,0:T(8,128)(2,1)S(1)}, bf16[4,4,32,256]{3,2,1,0:T(8,128)(2,1)}, u32[]{:S(2)}) copy-start(bf16[4,4,32,256]{3,2,1,0:T(8,128)(2,1)} %copy-done.2) | copy-start | bytes 786436 | tf_op jit(solution)/shard_map/cond
  46.4 9.8 %collective-permute-start.13 = (bf16[4,4,32,256]{3,2,1,0:T(8,128)(2,1)S(1)}, bf16[4,4,32,256]{3,2,1,0:T(8,128)(2,1)S(1)}, u32[]{:S(2)}, u32[]{:S(2)}) collective-permute-start(bf16[4,4,32,256]{3,2,1,0:T(8,128)(2,1)S(1)} %pad_maximum_fusion.b0), channel_id=1, source_target_pairs={{0,4},{4,0},{8,12},{12,8},{16,20},{20,16},{24,28},{28,24},{32,36},... | collective-permute-start | bytes 786440 | tf_op jit(solution)/shard_map/cond/branch_1_fun/ppermute | solution.py:512
  51.8 5.4 %collective-permute-start.14 = (bf16[4,4,32,256]{3,2,1,0:T(8,128)(2,1)S(1)}, bf16[4,4,32,256]{3,2,1,0:T(8,128)(2,1)S(1)}, u32[]{:S(2)}, u32[]{:S(2)}) collective-permute-start(bf16[4,4,32,256]{3,2,1,0:T(8,128)(2,1)S(1)} %collective-permute-done.3.b1), channel_id=1, source_target_pairs={{0,4},{4,0},{8,12},{12,8},{16,20},{20,16},{24,28},{28,24},{32,36},... | collective-permute-start | bytes 786440 | tf_op jit(solution)/shard_map/cond/branch_1_fun/ppermute | solution.py:512
  51.8 5.4 %collective-permute-start.15 = (bf16[4,4,32,256]{3,2,1,0:T(8,128)(2,1)S(1)}, bf16[4,4,32,256]{3,2,1,0:T(8,128)(2,1)S(1)}, u32[]{:S(2)}, u32[]{:S(2)}) collective-permute-start(bf16[4,4,32,256]{3,2,1,0:T(8,128)(2,1)S(1)} %collective-permute-done.4.b2), channel_id=1, source_target_pairs={{0,4},{4,0},{8,12},{12,8},{16,20},{20,16},{24,28},{28,24},{32,36},... | collective-permute-start | bytes 786440 | tf_op jit(solution)/shard_map/cond/branch_1_fun/ppermute | solution.py:512
  52.3 4.9 %collective-permute-start.16 = (bf16[4,4,32,256]{3,2,1,0:T(8,128)(2,1)S(1)}, bf16[4,4,32,256]{3,2,1,0:T(8,128)(2,1)S(1)}, u32[]{:S(2)}, u32[]{:S(2)}) collective-permute-start(bf16[4,4,32,256]{3,2,1,0:T(8,128)(2,1)S(1)} %collective-permute-done.5.b3), channel_id=1, source_target_pairs={{0,4},{4,0},{8,12},{12,8},{16,20},{20,16},{24,28},{28,24},{32,36},... | collective-permute-start | bytes 786440 | tf_op jit(solution)/shard_map/cond/branch_1_fun/ppermute | solution.py:512
  52.3 27.7 %collective-permute-start.18 = (f32[1024,128]{1,0:T(8,128)S(1)}, f32[1024,128]{1,0:T(8,128)S(1)}, u32[]{:S(2)}, u32[]{:S(2)}) collective-permute-start(f32[1024,128]{1,0:T(8,128)S(1)} %get-tuple-element.84), channel_id=1, source_target_pairs={{0,2},{1,3},{2,0},{3,1},{4,6},{5,7},{6,4},{7,5},{8,10},{9,11},{10,... | collective-permute-start | bytes 1572872 | tf_op jit(solution)/shard_map/cond/branch_1_fun/ppermute | solution.py:526
  56.2 23.8 %collective-permute-start.17 = (f32[1024,128]{1,0:T(8,128)S(1)}, f32[1024,128]{1,0:T(8,128)S(1)}, u32[]{:S(2)}, u32[]{:S(2)}) collective-permute-start(f32[1024,128]{1,0:T(8,128)S(1)} %get-tuple-element.89), channel_id=1, source_target_pairs={{0,1},{1,2},{2,3},{3,0},{4,5},{5,6},{6,7},{7,4},{8,9},{9,10},{10,1... | collective-permute-start | bytes 1572872 | tf_op jit(solution)/shard_map/cond/branch_1_fun/ppermute | solution.py:526
  60.7 32.5 %copy-start.6 = (bf16[8,8,32,256]{3,2,1,0:T(8,128)(2,1)S(1)}, bf16[8,8,32,256]{3,2,1,0:T(8,128)(2,1)}, u32[]{:S(2)}) copy-start(bf16[8,8,32,256]{3,2,1,0:T(8,128)(2,1)} %get-tuple-element.95.int_ref) | copy-start | bytes 3145732 | tf_op jit(solution)/shard_map/cond
  60.7 32.5 %copy-start.13 = (s32[8]{0:T(128)S(1)}, s32[8]{0:T(128)}, u32[]{:S(2)}) copy-start(s32[8]{0:T(128)} %get-tuple-element.70.sj_ref) | copy-start | bytes 100 | tf_op jit(solution)/shard_map/cond
  60.7 32.5 %copy-start.14 = (f32[1024]{0:T(1024)S(1)}, f32[1024]{0:T(1024)}, u32[]{:S(2)}) copy-start(f32[1024]{0:T(1024)} %get-tuple-element.73) | copy-start | bytes 12292 | tf_op jit(solution)/shard_map/cond
  60.7 32.5 %copy-start.16 = (f32[200]{0:T(256)S(1)}, f32[200]{0:T(256)}, u32[]{:S(2)}) copy-start(f32[200]{0:T(256)} %get-tuple-element.71.oe_ref) | copy-start | bytes 2404 | tf_op jit(solution)/shard_map/cond
  60.7 20.0 %collective-permute-start.19 = (f32[1024,128]{1,0:T(8,128)S(1)}, f32[1024,128]{1,0:T(8,128)S(1)}, u32[]{:S(2)}, u32[]{:S(2)}) collective-permute-start(f32[1024,128]{1,0:T(8,128)S(1)} %get-tuple-element.90), channel_id=1, source_target_pairs={{0,3},{1,0},{2,1},{3,2},{4,7},{5,4},{6,5},{7,6},{8,11},{9,8},{10,9... | collective-permute-start | bytes 1572872 | tf_op jit(solution)/shard_map/cond/branch_1_fun/ppermute | solution.py:526
  81.1 8.4 %collective-permute-start.20 = (f32[8,32,128]{2,1,0:T(8,128)S(1)}, f32[8,32,128]{2,1,0:T(8,128)S(1)}, u32[]{:S(2)}, u32[]{:S(2)}) collective-permute-start(f32[8,32,128]{2,1,0:T(8,128)S(1)} %get-tuple-element.92), channel_id=1, source_target_pairs={{0,24},{4,28},{8,0},{12,4},{16,8},{20,12},{24,16},{28,20},{32,56},... | collective-permute-start | bytes 393224 | tf_op jit(solution)/shard_map/cond/branch_1_fun/ppermute | solution.py:538
  84.1 7.8 %collective-permute-start.21 = (f32[8,32,128]{2,1,0:T(8,128)S(1)}, f32[8,32,128]{2,1,0:T(8,128)S(1)}, u32[]{:S(2)}, u32[]{:S(2)}) collective-permute-start(f32[8,32,128]{2,1,0:T(8,128)S(1)} %get-tuple-element.93), channel_id=1, source_target_pairs={{0,16},{4,20},{8,24},{12,28},{16,0},{20,4},{24,8},{28,12},{32,48},... | collective-permute-start | bytes 393224 | tf_op jit(solution)/shard_map/cond/branch_1_fun/ppermute | solution.py:538
  84.9 8.3 %collective-permute-start.22 = (f32[8,32,128]{2,1,0:T(8,128)S(1)}, f32[8,32,128]{2,1,0:T(8,128)S(1)}, u32[]{:S(2)}, u32[]{:S(2)}) collective-permute-start(f32[8,32,128]{2,1,0:T(8,128)S(1)} %get-tuple-element.94), channel_id=1, source_target_pairs={{0,8},{4,12},{8,16},{12,20},{16,24},{20,28},{24,0},{28,4},{32,40},... | collective-permute-start | bytes 393224 | tf_op jit(solution)/shard_map/cond/branch_1_fun/ppermute | solution.py:538
